TPU v7x, 32 devices: a whole 2x2x4 slice. The times are simulated.
32 devices in a mesh: dp: 16 (over z, y, x), seq: 2 (over core).
Axes of the slice: x: 2, y: 2, z: 4, core: 2. Of those that a mesh axis runs over, the one named last changes fastest.
Arguments:
- latents: bfloat16 [16, 1024, 1152], P('dp', 'seq'), may hold values from -6 to 6
- condition: bfloat16 [16, 1152], P('dp'), may hold values from -6 to 6
- cotangent: bfloat16 [16, 1024, 1152], P('dp', 'seq'), may hold values from -6 to 6
- teacher: bfloat16 [16, 1024, 1152], P('dp', 'seq'), may hold values from -6 to 6
- valid_mask: int32 [16, 1024], P('dp', 'seq'), may hold values from 0 to 1, as said below
- modulation_weight: float32 [1152, 6912], P('seq', 'dp'), may hold values from -0.1875 to 0.1875
- attention_weight: float32 [1152, 3456], P('seq', 'dp'), may hold values from -0.1875 to 0.1875
- projection_weight: float32 [1152, 1152], P('seq', 'dp'), may hold values from -0.5 to 0.5
- expansion_weight: float32 [1152, 4608], P('seq', 'dp'), may hold values from -0.1875 to 0.1875
- contraction_weight: float32 [4608, 1152], P('seq', 'dp'), may hold values from -0.125 to 0.125
- modulation_moment: float32 [1152, 6912], P('seq', 'dp'), may hold values from -224 to 224
- attention_moment: float32 [1152, 3456], P('seq', 'dp'), may hold values from -80 to 80
- projection_moment: float32 [1152, 1152], P('seq', 'dp'), may hold values from -160 to 160
- expansion_moment: float32 [1152, 4608], P('seq', 'dp'), may hold values from -224 to 224
- contraction_moment: float32 [4608, 1152], P('seq', 'dp'), may hold values from -320 to 320
- modulation_average: float32 [1152, 6912], P('seq', 'dp'), may hold values from -0.1875 to 0.1875
- attention_average: float32 [1152, 3456], P('seq', 'dp'), may hold values from -0.1875 to 0.1875
- projection_average: float32 [1152, 1152], P('seq', 'dp'), may hold values from -0.5 to 0.5
- expansion_average: float32 [1152, 4608], P('seq', 'dp'), may hold values from -0.1875 to 0.1875
- contraction_average: float32 [4608, 1152], P('seq', 'dp'), may hold values from -0.125 to 0.125
Outputs:
- block_output: float32 [16, 1024, 1152], P('dp', 'seq')
- masked_loss: float32 [], replicated
- latent_grad: float32 [16, 1024, 1152], P('dp', 'seq')
- condition_grad: float32 [16, 1152], P('dp')
- modulation_next: float32 [1152, 6912], P('seq', 'dp')
- attention_next: float32 [1152, 3456], P('seq', 'dp')
- projection_next: float32 [1152, 1152], P('seq', 'dp')
- expansion_next: float32 [1152, 4608], P('seq', 'dp')
- contraction_next: float32 [4608, 1152], P('seq', 'dp')
- modulation_moment_next: float32 [1152, 6912], P('seq', 'dp')
- attention_moment_next: float32 [1152, 3456], P('seq', 'dp')
- projection_moment_next: float32 [1152, 1152], P('seq', 'dp')
- expansion_moment_next: float32 [1152, 4608], P('seq', 'dp')
- contraction_moment_next: float32 [4608, 1152], P('seq', 'dp')
- modulation_average_next: float32 [1152, 6912], P('seq', 'dp')
- attention_average_next: float32 [1152, 3456], P('seq', 'dp')
- projection_average_next: float32 [1152, 1152], P('seq', 'dp')
- expansion_average_next: float32 [1152, 4608], P('seq', 'dp')
- contraction_average_next: float32 [4608, 1152], P('seq', 'dp')
Inputs may be any that keep to these rules, and one draw needn't show every extreme that they name: `valid_mask`: the first token of every latent is valid.
All inputs are finite; a program needn't handle non-finite values.
Results may differ from a plain program's by a relative error of at most 0.02.
The roundings to bfloat16 on the way count: a program that leaves them out, or rounds other values in their place, can miss the bound.
Values may be sent and summed in bfloat16 or wider, within the bound.
No kernel may reach another device: no remote copies, remote signals or barrier semaphores. Data moves between devices by JAX's collectives and lax.ppermute only.
A program may use at most 320 MiB of HBM per device.

v0:
```python
import math

import jax
import jax.numpy as jnp
from jax import lax
from jax.experimental import pallas as pl
from jax.experimental.pallas import tpu as pltpu
from jax.sharding import PartitionSpec as P

HEADS = 16
SEQ_LEN = 1024

epsilon = 1e-06
log2_e = math.log2(math.e)
low = jnp.bfloat16


def silu_of(values):
    return values * jax.nn.sigmoid(values)


def gelu_of(values):
    square = values * values
    tanh = jnp.tanh(values * (0.7978845608028654 + (0.044715 * 0.7978845608028654) * square))
    half = 0.5 * tanh + 0.5
    value = values * half
    inner = 2 * 0.7978845608028654 + (6 * 0.044715 * 0.7978845608028654) * square
    return value, half + (value - value * half) * inner


def modulated(values, offset, stretch):
    centered = values - jnp.mean(values, axis=-1, keepdims=True)
    variance = jnp.mean(centered * centered, axis=-1, keepdims=True)
    return centered * lax.rsqrt(variance + epsilon) * (1.0 + stretch) + offset


def dot(first, second, over):
    return lax.dot_general(first, second, (over, ((), ())), preferred_element_type=jnp.float32)


def nn(first, second):
    return dot(first, second, ((1,), (0,)))


def nt(first, second):
    return dot(first, second, ((1,), (1,)))


def tn(first, second):
    return dot(first, second, ((0,), (0,)))


def around(pieces):
    size = lax.axis_size("seq")
    got = [pieces[0]] * size
    for r in range(1, size):
        steps = [(j, (j + r) % size) for j in range(size)]
        got[(size - r) % size] = lax.ppermute(pieces[r], "seq", steps)
    return got


def in_order(got):
    size = lax.axis_size("seq")
    me = lax.axis_index("seq")
    if size == 2:
        return [jnp.where(me == 0, got[0], got[1]), jnp.where(me == 0, got[1], got[0])]
    stacked = jnp.stack(got)
    return [lax.dynamic_index_in_dim(stacked, (j - me) % size, 0, False) for j in range(size)]


def by_distance(array, axis):
    size = lax.axis_size("seq")
    me = lax.axis_index("seq")
    return [lax.dynamic_index_in_dim(array, (me + r) % size, axis, False) for r in range(size)]


def gather_tokens(own):
    return lax.optimization_barrier(
        jnp.concatenate(around([own] * lax.axis_size("seq")), axis=0)
    )


def sum_tokens(parts):
    got = around(parts[:1] + [lax.optimization_barrier(part) for part in parts[1:]])
    return sum([lax.optimization_barrier(got[0])] + got[1:])


def swap(array, bit):
    size = lax.axis_size("dp")
    return lax.ppermute(array, "dp", [(j, j ^ bit) for j in range(size)])


def hypercube():
    size = lax.axis_size("dp")
    return size >= 4 and size & (size - 1) == 0


nothing = pl.CostEstimate(flops=0, bytes_accessed=0, transcendentals=0)
in_hbm = pl.BlockSpec(memory_space=pltpu.HBM)


def after(value, *others):
    def kernel(*refs):
        pass

    if not others:
        return value
    return pl.pallas_call(
        kernel,
        out_shape=jax.ShapeDtypeStruct(value.shape, value.dtype),
        in_specs=[in_hbm] * (1 + len(others)),
        out_specs=in_hbm,
        input_output_aliases={0: 0},
        cost_estimate=nothing,
    )(value, *others)


def place(*ways):
    size = lax.axis_size("dp")
    count = len(ways)
    me = lax.axis_index("dp").astype(jnp.int32)
    index = (jnp.array([steps for _, steps in ways], jnp.int32) ^ me) & 3

    def kernel(index_ref, *refs):
        sources, targets = refs[: 4 * count], refs[4 * count : 5 * count]
        held, (arrived, left) = refs[5 * count : 6 * count], refs[6 * count :]
        inward, outward = [], []
        for n in range(4):
            for w in range(count):
                copy = pltpu.make_async_copy(sources[4 * w + n], held[w].at[n], arrived.at[w, n])
                copy.start()
                inward.append(copy)
        for n in range(4):
            for w in range(count):
                inward[n * count + w].wait()
                target = targets[w].at[:, index_ref[w, n]]
                copy = pltpu.make_async_copy(held[w].at[n], target, left.at[w, n])
                copy.start()
                outward.append(copy)
        for copy in outward:
            copy.wait()

    groups = [pieces[0].shape for pieces, _ in ways]
    placed = pl.pallas_call(
        kernel,
        out_shape=[jax.ShapeDtypeStruct((g[0], 4) + g[1:], low) for g in groups],
        in_specs=[pl.BlockSpec(memory_space=pltpu.SMEM)] + [in_hbm] * (4 * count),
        out_specs=[in_hbm] * count,
        scratch_shapes=[pltpu.VMEM((4,) + g, low) for g in groups]
        + [pltpu.SemaphoreType.DMA((count, 4))] * 2,
        compiler_params=pltpu.CompilerParams(vmem_limit_bytes=24 << 20),
        cost_estimate=nothing,
    )(index, *[piece for pieces, _ in ways for piece in pieces])
    return [whole.reshape((size,) + whole.shape[2:]) for whole in placed]


def gather_high(shard):
    if not hypercube():
        return shard
    held, bit = shard[None], lax.axis_size("dp") >> 1
    while bit >= 4:
        came = swap(held, bit)
        upper = (lax.axis_index("dp") & bit) != 0
        pair = [jnp.where(upper, came, held), jnp.where(upper, held, came)]
        held = jnp.stack(pair, axis=1).reshape((-1,) + held.shape[1:])
        bit >>= 1
    return held


class Low:
    def __init__(self, held, first, last):
        self.held, self.first, self.last = held, first, last
        if not hypercube():
            self.all = lax.all_gather(held, "dp", axis=0)
            return
        self.by_first = swap(held, first)
        self.by_last = swap(held, last)
        self.by_both = swap(self.by_first, last)

    def pieces(self):
        steps = (0, self.first, self.last, self.first | self.last)
        return [self.held, self.by_first, self.by_last, self.by_both], steps


def wholes(*ways):
    if not hypercube():
        return [way.all for way in ways]
    return place(*[way.pieces() for way in ways])


def plus(*parts):
    return sum(part.astype(jnp.float32) for part in parts).astype(parts[0].dtype)


class Sum:
    def __init__(self, blocks, first, last):
        self.blocks, self.first, self.last = blocks, first, last
        size = lax.axis_size("dp")
        if not hypercube():
            self.sent = []
            return
        me = lax.axis_index("dp")

        def group(distance):
            want = (me ^ distance) & 3
            parts = []
            for block in blocks:
                shape = block.shape[1:]
                part = lax.dynamic_slice(
                    block.reshape((size // 4, 2, 2) + shape),
                    (0, want >> 1, want & 1) + (0,) * len(shape),
                    (size // 4, 1, 1) + shape,
                )
                parts.append(part.reshape((size // 4,) + shape))
            return jnp.concatenate(parts, axis=1)

        self.sent = [group(first | last), group(first)]
        self.far = swap(self.sent[0], first)
        self.near = swap(self.sent[1], first)
        self.kept = group(last), group(0)

    def second(self, *others):
        self.passed = []
        if hypercube():
            self.onward = plus(self.kept[0], after(self.far, *others))
            self.passed = [self.onward]

    def third(self, *others):
        self.held = []
        if hypercube():
            through = swap(after(self.onward, *others), self.last)
            self.total = plus(self.kept[1], self.near, through)
            self.held = [self.total]

    def finish(self, *waits):
        if not hypercube():
            blocks = jnp.concatenate(self.blocks, axis=1)
            return lax.psum_scatter(blocks, "dp", scatter_dimension=0, tiled=False)
        waits = list(waits)

        def came(array):
            return after(array, *waits.pop(0)) if waits else array

        me = lax.axis_index("dp")
        held, bit = self.total, 4
        while bit < lax.axis_size("dp"):
            pairs = held.reshape((held.shape[0] // 2, 2) + held.shape[1:])
            mine = (me // bit) & 1
            away = lax.dynamic_index_in_dim(pairs, 1 - mine, 1, False)
            held = plus(lax.dynamic_index_in_dim(pairs, mine, 1, False), came(swap(away, bit)))
            bit <<= 1
        return held[0]


def gather_small(own, *others):
    size = lax.axis_size("dp")
    if not hypercube():
        return lax.all_gather(own, "dp", axis=0)
    me = lax.axis_index("dp")
    held, bit = own[None], 1
    while bit < size:
        came = swap(held, bit)
        upper = (me & bit) != 0
        held = jnp.concatenate(
            [jnp.where(upper, came, held), jnp.where(upper, held, came)], axis=0
        )
        bit <<= 1
        if bit == 4:
            held = after(held, *others)
    return held


def sum_small(blocks):
    return jnp.sum(lax.all_to_all(blocks, "dp", 0, 0, tiled=True), axis=0)


def softmax_kernel(heads, head_size, block, qkv_ref, out_ref, low_ref, log_ref, key_ref, value_ref):
    width, length = heads * head_size, qkv_ref.shape[1]
    for h in range(heads):
        cols = slice(h * head_size, (h + 1) * head_size)
        key_ref[...] = qkv_ref[0, :, width + h * head_size : width + (h + 1) * head_size]
        value_ref[...] = qkv_ref[0, :, 2 * width + h * head_size : 2 * width + (h + 1) * head_size]
        for b in range(length // block):
            rows = slice(b * block, (b + 1) * block)
            scores = nt(qkv_ref[0, rows, cols], key_ref[...]) * (head_size ** (-0.5) * log2_e)
            top = jnp.max(scores, axis=1, keepdims=True)
            raised = jnp.exp2(scores - top)
            total = jnp.sum(raised, axis=1, keepdims=True)
            out = nn(raised.astype(low), value_ref[...]) / total
            out_ref[0, rows, cols] = out
            low_ref[0, rows, cols] = out.astype(low)
            log_ref[0, h : h + 1, rows] = (top + jnp.log2(total)).T


def one_latent(*shape):
    return pl.BlockSpec((1,) + shape, lambda i: (i, 0, 0))


def attend(qkv, heads, head_size):
    latents, length, columns = qkv.shape
    width = heads * head_size
    return pl.pallas_call(
        lambda *refs: softmax_kernel(heads, head_size, math.gcd(length, 256), *refs),
        out_shape=(
            jax.ShapeDtypeStruct((latents, length, width), jnp.float32),
            jax.ShapeDtypeStruct((latents, length, width), low),
            jax.ShapeDtypeStruct((latents, heads, length), jnp.float32),
        ),
        grid=(latents,),
        in_specs=[one_latent(length, columns)],
        out_specs=(
            one_latent(length, width),
            one_latent(length, width),
            one_latent(heads, length),
        ),
        scratch_shapes=[pltpu.VMEM((length, head_size), low)] * 2,
        compiler_params=pltpu.CompilerParams(vmem_limit_bytes=48 << 20),
        cost_estimate=pl.CostEstimate(
            flops=4 * latents * length * length * width,
            bytes_accessed=10 * latents * heads * length * length,
            transcendentals=latents * heads * length * length,
        ),
    )(qkv)


def softmax_back_kernel(
    heads,
    head_size,
    block,
    qkv_ref,
    grad_ref,
    out_ref,
    log_ref,
    qkv_grad_ref,
    key_ref,
    value_ref,
    key_sum,
    value_sum,
):
    width, length = heads * head_size, qkv_ref.shape[1]
    scale = head_size ** (-0.5)
    for h in range(heads):
        cols = slice(h * head_size, (h + 1) * head_size)
        key_cols = slice(width + h * head_size, width + (h + 1) * head_size)
        value_cols = slice(2 * width + h * head_size, 2 * width + (h + 1) * head_size)
        key_ref[...] = qkv_ref[0, :, key_cols]
        value_ref[...] = qkv_ref[0, :, value_cols]
        for b in range(length // block):
            rows = slice(b * block, (b + 1) * block)
            query, grad = qkv_ref[0, rows, cols], grad_ref[0, rows, cols]
            delta = jnp.sum(
                (grad.astype(jnp.float32) * out_ref[0, rows, cols]).T, axis=0, keepdims=True
            )
            probability = jnp.exp2(
                nt(key_ref[...], query) * (scale * log2_e) - log_ref[0, h : h + 1, rows]
            )
            score_grad = (probability * (nt(value_ref[...], grad) - delta)).astype(low)
            key_part = nn(score_grad, query)
            value_part = nn(probability.astype(low), grad)
            key_sum[...] = key_part if b == 0 else key_sum[...] + key_part
            value_sum[...] = value_part if b == 0 else value_sum[...] + value_part
            qkv_grad_ref[0, rows, cols] = (tn(score_grad, key_ref[...]) * scale).astype(low)
        qkv_grad_ref[0, :, key_cols] = (key_sum[...] * scale).astype(low)
        qkv_grad_ref[0, :, value_cols] = value_sum[...].astype(low)


def attend_back(qkv, grad, out, log_total, heads, head_size):
    latents, length, columns = qkv.shape
    width = heads * head_size
    return pl.pallas_call(
        lambda *refs: softmax_back_kernel(heads, head_size, math.gcd(length, 512), *refs),
        out_shape=jax.ShapeDtypeStruct((latents, length, columns), low),
        grid=(latents,),
        in_specs=[
            one_latent(length, columns),
            one_latent(length, width),
            one_latent(length, width),
            one_latent(heads, length),
        ],
        out_specs=one_latent(length, columns),
        scratch_shapes=[pltpu.VMEM((length, head_size), low)] * 2
        + [pltpu.VMEM((length, head_size), jnp.float32)] * 2,
        compiler_params=pltpu.CompilerParams(vmem_limit_bytes=56 << 20),
        cost_estimate=nothing,
    )(qkv, grad, out, log_total)


def body(
    latents,
    condition,
    cotangent,
    teacher,
    valid_mask,
    modulation_weight,
    attention_weight,
    projection_weight,
    expansion_weight,
    contraction_weight,
    modulation_moment,
    attention_moment,
    projection_moment,
    expansion_moment,
    contraction_moment,
    modulation_average,
    attention_average,
    projection_average,
    expansion_average,
    contraction_average,
):
    local_latents, block_rows, width = latents.shape
    seq_size, dp_size = lax.axis_size("seq"), lax.axis_size("dp")
    seq_me, dp_me = lax.axis_index("seq"), lax.axis_index("dp")
    all_latents = local_latents * dp_size
    head_size = width // HEADS
    heads = HEADS // seq_size
    own_width = heads * head_size
    score_scale = head_size ** (-0.5)
    own_tokens = local_latents * block_rows
    tokens = own_tokens * seq_size
    row_share = attention_weight.shape[0]
    mod_share = modulation_weight.shape[1]
    qkv_share = attention_weight.shape[1]
    proj_share = projection_weight.shape[1]
    hidden_share = expansion_weight.shape[1]
    hidden_piece = hidden_share // seq_size

    row_room = (row_share + 127) // 128 * 128

    def roomy(array):
        return jnp.pad(array, [(0, 0)] * (array.ndim - 1) + [(0, row_room - array.shape[-1])])

    attention_low = roomy(attention_weight.astype(low).T)
    expansion_low = after(expansion_weight.astype(low).T, attention_low)
    expansion_low = expansion_low.reshape(seq_size, hidden_piece, row_share)
    expansion_shard = jnp.concatenate(in_order(around(by_distance(expansion_low, 0))), axis=1)
    contraction_low = after(contraction_weight.astype(low), attention_low).reshape(
        dp_size // seq_size, seq_size, hidden_piece, proj_share
    )
    contraction_shard = jnp.concatenate(in_order(around(by_distance(contraction_low, 1))), axis=0)
    contraction_shard = contraction_shard.reshape(dp_size * hidden_piece, proj_share).T
    projection_low = projection_weight.astype(low).T

    def widen(shard):
        rows, columns = shard.shape
        if columns >= width:
            return jnp.concatenate(jnp.split(shard, columns // width, axis=1), axis=0)
        return jnp.concatenate(jnp.split(shard, width // columns, axis=0), axis=1)

    def narrow(wide, rows):
        if wide.shape[-2] >= rows:
            return jnp.concatenate(jnp.split(wide, wide.shape[-2] // rows, axis=-2), axis=-1)
        return jnp.concatenate(jnp.split(wide, rows // wide.shape[-2], axis=-1), axis=-2)

    def widen_blocks(blocks):
        return jax.vmap(widen)(blocks)

    rides = width % own_width == 0 and proj_share % (width // own_width) == 0
    one = [widen(contraction_shard), expansion_shard]
    if rides:
        one.append(widen(projection_low))
    cut_c = one[0].shape[0]
    cut_e = cut_c + hidden_piece
    one_full = lax.all_gather(jnp.concatenate(one, axis=0), "dp", axis=0)
    if not rides:
        projection_full = lax.all_gather(projection_low, "dp", axis=0)

    attention_high = gather_high(attention_low)
    first_ready = [attention_high]
    half = (qkv_share // 2 + 15) // 16 * 16
    attention_a = Low(attention_high[..., :half, :], 1, 2)
    attention_b = Low(attention_high[..., half:, :], 2, 1)

    mask_float = valid_mask.astype(jnp.float32)
    chunk = math.gcd(own_tokens, 128)
    counts = jnp.sum(mask_float.reshape(own_tokens // chunk, chunk), axis=1).astype(low)
    packed = jnp.concatenate([condition.reshape(-1), counts])
    packed = gather_small(jnp.stack(in_order(around([packed] * seq_size))), *first_ready)
    count_total = jnp.sum(packed[:, :, local_latents * width :].astype(jnp.float32))
    every_cond = packed[:, 0, : local_latents * width].reshape(all_latents, width)
    cond_active = silu_of(every_cond.astype(jnp.float32)).astype(low)
    cond_rows = lax.dynamic_slice(
        cond_active, (0, seq_me * row_share), (all_latents, row_share)
    )
    attention_rows = jnp.concatenate(wholes(attention_a, attention_b), axis=1)
    attention_rows = attention_rows.reshape(3, seq_size, own_width, row_room)
    attention_full = jnp.concatenate(
        in_order(around(by_distance(attention_rows, 1))), axis=-1
    ).reshape(3 * own_width, seq_size * row_room)

    modulation_low = modulation_weight.astype(low)
    mod_part = nn(cond_rows, modulation_low).reshape(dp_size, local_latents, mod_share)
    mod_part = lax.all_to_all(mod_part, "dp", 0, 0, tiled=True)
    modulation = sum(around([mod_part] * seq_size))
    modulation = jnp.transpose(modulation, (1, 0, 2)).reshape(local_latents, dp_size * mod_share)
    shift_attn, scale_attn, gate_attn, shift_mlp, scale_mlp, gate_mlp = [
        group[:, None, :] for group in jnp.split(modulation, 6, axis=-1)
    ]

    residual_in = latents.astype(jnp.float32)
    attn_value, attn_pull = jax.vjp(modulated, residual_in, shift_attn, scale_attn)
    attn_input = roomy(attn_value.astype(low).reshape(own_tokens, seq_size, row_share))
    attn_input = gather_tokens(attn_input.reshape(own_tokens, seq_size * row_room))
    qkv_low = nt(attn_input, attention_full).astype(low)

    def by_latent(array):
        array = array.reshape(seq_size, local_latents, block_rows, -1)
        return jnp.transpose(array, (1, 0, 2, 3)).reshape(
            local_latents, seq_size * block_rows, -1
        )

    def by_device(array):
        array = array.reshape(local_latents, seq_size, block_rows, -1)
        return jnp.transpose(array, (1, 0, 2, 3)).reshape(tokens, -1)

    qkv = by_latent(qkv_low)
    attn_out, attn_low, log_total = attend(qkv, heads, head_size)
    attn_low = by_device(attn_low)

    one_full = after(one_full, attn_low)
    contraction_full = narrow(one_full[:, :cut_c], proj_share).reshape(
        width, dp_size * hidden_piece
    )
    expansion_full = one_full[:, cut_c:cut_e].reshape(dp_size * hidden_piece, width)
    if rides:
        projection_full = narrow(one_full[:, cut_e:], proj_share)
    projection_full = projection_full.reshape(width, own_width)

    def by_block(array):
        return [array[r * own_tokens : (r + 1) * own_tokens] for r in range(seq_size)]

    def own_shape(array):
        return array.reshape(local_latents, block_rows, width)

    proj_out = own_shape(sum_tokens([nt(rows, projection_full) for rows in by_block(attn_low)]))
    mid_resid = residual_in + gate_attn * proj_out

    mlp_value, mlp_pull = jax.vjp(modulated, mid_resid, shift_mlp, scale_mlp)
    mlp_input = gather_tokens(mlp_value.astype(low).reshape(own_tokens, width))
    value, slope = gelu_of(nt(mlp_input, expansion_full))
    hidden_low, hidden_slope = lax.optimization_barrier((value.astype(low), slope.astype(low)))
    mlp_out = own_shape(sum_tokens([nt(rows, contraction_full) for rows in by_block(hidden_low)]))
    block_output = mid_resid + gate_mlp * mlp_out

    teacher_gap = block_output - teacher.astype(jnp.float32)
    local_square = jnp.sum(mask_float[..., None] * teacher_gap * teacher_gap)
    out_grad = cotangent.astype(jnp.float32) + 2.0 * mask_float[..., None] * teacher_gap / (
        count_total * width
    )

    gate_mlp_grad = jnp.sum(out_grad * mlp_out, axis=1)
    mlp_out_grad = gather_tokens((gate_mlp * out_grad).astype(low).reshape(own_tokens, width))
    folds = max(dp_size * hidden_piece // width, 1)
    contraction_grad = [
        tn(mlp_out_grad, part).astype(low).reshape(dp_size, proj_share, -1)
        for part in jnp.split(hidden_low, folds, axis=1)
    ]
    hidden_grad = nn(mlp_out_grad, contraction_full)
    hidden_pre_grad = (hidden_grad * hidden_slope.astype(jnp.float32)).astype(low)
    expansion_grad = tn(hidden_pre_grad, mlp_input).astype(low)
    expansion_grad = expansion_grad.reshape(dp_size, hidden_piece, width)
    if contraction_grad[0].shape[-1] != width:
        contraction_grad = [widen_blocks(part) for part in contraction_grad]
    mlp_grads = jnp.concatenate(contraction_grad + [expansion_grad], axis=1)
    expansion_back = after(expansion_full, mlp_grads)
    mlp_sum = lax.psum_scatter(mlp_grads, "dp", scatter_dimension=0, tiled=False)
    if cut_c == seq_size * proj_share:
        contraction_sum = by_distance(mlp_sum[:cut_c].reshape(seq_size, proj_share, width), 0)
    else:
        contraction_sum = narrow(mlp_sum[:cut_c], proj_share).reshape(proj_share, seq_size, -1)
        contraction_sum = by_distance(contraction_sum, 1)
    expansion_sum = mlp_sum[cut_c:]
    mlp_input_grad = own_shape(
        sum_tokens([nn(rows, expansion_back) for rows in by_block(hidden_pre_grad)])
    )
    mid_part, shift_mlp_grad, scale_mlp_grad = mlp_pull(mlp_input_grad)
    mid_grad = out_grad + mid_part

    gate_attn_grad = jnp.sum(mid_grad * proj_out, axis=1)
    proj_out_grad = gather_tokens((gate_attn * mid_grad).astype(low).reshape(own_tokens, width))
    projection_grad = tn(proj_out_grad, roomy(attn_low)).astype(low)
    attn_out_grad = by_latent(nn(proj_out_grad, projection_full).astype(low))
    qkv_grad = by_device(
        attend_back(qkv, attn_out_grad, attn_out, log_total, heads, head_size)
    )
    features = attn_input.reshape(tokens, seq_size, row_room)
    attention_grad = [
        tn(qkv_grad, columns).astype(low).reshape(3, own_width, row_room)
        for columns in by_distance(features, 1)
    ]
    attention_grad = jnp.stack(in_order(around(attention_grad)), axis=1).reshape(
        dp_size, qkv_share, row_room
    )
    projection_grad = projection_grad.reshape(dp_size, proj_share, row_room)
    sum_half = (qkv_share + proj_share) // 2
    attention_sum = [
        Sum([attention_grad[:, :sum_half]], 1, 2),
        Sum([attention_grad[:, sum_half:], projection_grad], 2, 1),
    ]
    qkv_grad = after(qkv_grad, *attention_sum[0].sent, *attention_sum[1].sent)
    attn_input_grad = sum_tokens([nn(rows, attention_full) for rows in by_block(qkv_grad)])
    attn_input_grad = attn_input_grad.reshape(own_tokens, seq_size, row_room)[..., :row_share]
    attn_input_grad = own_shape(attn_input_grad)
    resid_part, shift_attn_grad, scale_attn_grad = attn_pull(attn_input_grad)
    latent_grad = mid_grad + resid_part

    mod_grad = jnp.concatenate(
        [
            shift_attn_grad[:, 0, :],
            scale_attn_grad[:, 0, :],
            gate_attn_grad,
            shift_mlp_grad[:, 0, :],
            scale_mlp_grad[:, 0, :],
            gate_mlp_grad,
        ],
        axis=-1,
    )
    mod_local = mod_grad
    mod_grad = sum(around([mod_grad] * seq_size)).astype(low)
    mod_grad = jnp.transpose(mod_grad.reshape(local_latents, dp_size, mod_share), (1, 0, 2))
    mod_grad = lax.all_to_all(mod_grad, "dp", 0, 0, tiled=True).reshape(all_latents, mod_share)
    for part in attention_sum:
        part.second(mod_local)
    for part in attention_sum:
        part.third(mod_grad)
    modulation_sum = tn(cond_rows, mod_grad)
    cond_part = nt(mod_grad, modulation_low).reshape(dp_size, local_latents * row_share)
    squares = jnp.broadcast_to(local_square, (dp_size, 128))
    back = sum_small(jnp.concatenate([cond_part, squares], axis=1))[None]
    back = after(back, *attention_sum[0].held, *attention_sum[1].held)
    back = jnp.stack(in_order(around([back] * seq_size)), axis=0)
    square_total = jnp.sum(back[:, 0, local_latents * row_share])
    masked_loss = square_total / (count_total * width)
    cond_grad = back[:, 0, : local_latents * row_share].reshape(seq_size, local_latents, row_share)
    cond_grad = jnp.transpose(cond_grad, (1, 0, 2)).reshape(local_latents, width)
    silu_pull = jax.vjp(silu_of, condition.astype(jnp.float32))[1]
    condition_grad = silu_pull(cond_grad)[0]

    waits = ([back],)
    attention_sum = jnp.concatenate([part.finish(*waits) for part in attention_sum], axis=0)
    expansion_sum = around(
        by_distance(expansion_sum.reshape(hidden_piece, seq_size, row_share), 1)
    )
    expansion_sum = jnp.concatenate(in_order(expansion_sum), axis=0).T
    contraction_sum = jnp.stack(in_order(around(contraction_sum)), axis=0).reshape(
        seq_size, proj_share, dp_size // seq_size, hidden_piece
    )
    contraction_sum = jnp.transpose(contraction_sum, (2, 0, 3, 1)).reshape(
        contraction_weight.shape
    )
    gradients = (
        modulation_sum,
        attention_sum[:qkv_share, :row_share].astype(jnp.float32).T,
        attention_sum[qkv_share:, :row_share].astype(jnp.float32).T,
        expansion_sum.astype(jnp.float32),
        contraction_sum.astype(jnp.float32),
    )

    step_rate = 0.06 / math.sqrt(all_latents * SEQ_LEN)
    masters = (
        modulation_weight,
        attention_weight,
        projection_weight,
        expansion_weight,
        contraction_weight,
    )
    moments = (
        modulation_moment,
        attention_moment,
        projection_moment,
        expansion_moment,
        contraction_moment,
    )
    averages = (
        modulation_average,
        attention_average,
        projection_average,
        expansion_average,
        contraction_average,
    )
    weight_next = []
    moment_next = []
    average_next = []
    for master, gradient, moment, average in zip(masters, gradients, moments, averages):
        moment_new = 0.5 * moment + gradient
        master_new = master - step_rate * (gradient + 0.5 * moment_new)
        weight_next.append(master_new)
        moment_next.append(moment_new)
        average_next.append(0.5 * average + 0.5 * master_new)
    return (
        block_output,
        masked_loss,
        latent_grad,
        condition_grad,
        *weight_next,
        *moment_next,
        *average_next,
    )


def solution(mesh):
    tokens_spec = P("dp", "seq", None)
    weight_spec = P("seq", "dp")
    in_specs = (
        tokens_spec,
        P("dp", None),
        tokens_spec,
        tokens_spec,
        P("dp", "seq"),
    ) + (weight_spec,) * 15
    out_specs = (tokens_spec, P(), tokens_spec, P("dp", None)) + (weight_spec,) * 15
    return jax.shard_map(body, mesh=mesh, in_specs=in_specs, out_specs=out_specs, check_vma=False)
```

profile of v0, /device:TPU:0, one launch (start us, length us, event | category | flops | bytes accessed | tf_op | source)
XLA Modules:
  0.0 507.4 jit_solution(3190824489958514819)
XLA Ops:
  17.6 4.0 collective-permute-start.3
  27.0 12.8 %collective-permute-done.3 = bf16[1,216,640]{2,1,0:T(8,128)(2,1)S(1)} collective-permute-done((bf16[1,216,640]{2,1,0:T(8,128)(2,1)S(1)}, bf16[1,216,640]{2,1,0:T(8,128)(2,1)S(1)}, u32[]{:S(2)}, u32[]{:S(2)}) %collective-permute-start.3) | collective-permute-done | bytes 276512 | tf_op jit(solution)/shard_map/ppermute | solution.py:90
  40.0 4.9 collective-permute-start.4
  45.5 17.0 %collective-permute-done.4 = bf16[2,216,640]{2,1,0:T(8,128)(2,1)S(1)} collective-permute-done((bf16[2,216,640]{2,1,0:T(8,128)(2,1)S(1)}, bf16[2,216,640]{2,1,0:T(8,128)(2,1)S(1)}, u32[]{:S(2)}, u32[]{:S(2)}) %collective-permute-start.4) | collective-permute-done | bytes 552992 | tf_op jit(solution)/shard_map/ppermute | solution.py:90
  63.8 4.7 collective-permute-done.5
  69.4 4.2 collective-permute-start.6
  79.3 18.1 %collective-permute-done.9.refs_1_ = bf16[4,112,640]{2,1,0:T(8,128)(2,1)S(1)} collective-permute-done((bf16[4,112,640]{2,1,0:T(8,128)(2,1)S(1)}, bf16[4,112,640]{2,1,0:T(8,128)(2,1)S(1)}, u32[]{:S(2)}, u32[]{:S(2)}) %collective-permute-start.9) | collective-permute-done | bytes 573472 | tf_op jit(solution)/shard_map/ppermute | solution.py:90
  101.5 4.9 all-to-all-start
  108.4 5.4 %all-to-all-done = f32[16,1,432]{2,1,0:T(1,128)S(1)} async-done(((f32[16,1,432]{2,1,0:T(1,128)}), f32[16,1,432]{2,1,0:T(1,128)S(1)}, u32[]{:S(2)}, u32[]{:S(2)}) %all-to-all-start) | async-done | bytes 27680 | tf_op jit(solution)/shard_map/all_to_all | solution.py:492
  115.3 10.9 %collective-permute-done.14.refs_7_ = bf16[4,104,640]{2,1,0:T(8,128)(2,1)} collective-permute-done((bf16[4,104,640]{2,1,0:T(8,128)(2,1)S(1)}, bf16[4,104,640]{2,1,0:T(8,128)(2,1)}, u32[]{:S(2)}, u32[]{:S(2)}) %collective-permute-start.14) | collective-permute-done | bytes 532512 | tf_op jit(solution)/shard_map/ppermute | solution.py:90
  126.2 2.4 shard_map.349
  129.0 2.1 copy-done.16
  134.2 2.4 copy.170
  138.7 2.7 collective-permute-done.8
  141.8 3.0 bitcast_select_fusion.1
  145.1 2.0 copy-done.30
  147.2 6.7 %fusion.9.refs_0_ = bf16[1,1024,1728]{2,1,0:T(8,128)(2,1)} fusion(bf16[1024,1280]{0,1:T(8,128)(2,1)S(1)} %pad_maximum_fusion.5, bf16[1728,1280]{1,0:T(8,128)(2,1)S(1)} %bitcast.329), kind=kOutput, calls=%fused_computation.27 | convolution fusion | flops 4531617792 | bytes 10584064 | tf_op jit(solution)/shard_map/dot_general | solution.py:38
  153.9 22.3 %shard_map.350 = (f32[1,1024,576]{2,1,0:T(8,128)S(1)}, bf16[1,1024,576]{2,1,0:T(8,128)(2,1)S(1)}, f32[1,8,1024]{2,1,0:T(8,128)S(1)}) custom-call(bf16[1,1024,1728]{2,1,0:T(8,128)(2,1)} %fusion.9.refs_0_), custom_call_target="tpu_custom_call" | custom-call | flops 2415919104 | bytes 83886080 | tf_op jit(solution)/shard_map/pallas_call | solution.py:302
  179.4 10.0 %all-gather.4.cloned.1.call-done.refs_0_ = bf16[16,324,1152]{2,1,0:T(8,128)(2,1)} async-done(((bf16[1,324,1152]{2,1,0:T(8,128)(2,1)}), bf16[16,324,1152]{2,1,0:T(8,128)(2,1)}) %all-gather.4.cloned.1.call-update) | async-done | bytes 11943952 | tf_op jit(solution)/shard_map/all_gather | solution.py:463
  193.9 2.9 slice.108
  202.6 3.0 fusion.95
  205.5 2.9 pad_maximum_fusion.1
  208.6 10.6 %fusion.2 = (bf16[1024,2304]{1,0:T(8,128)(2,1)}, bf16[1024,2304]{1,0:T(8,128)(2,1)S(1)}) fusion(bf16[1024,1152]{1,0:T(8,128)(2,1)S(1)} %pad_maximum_fusion.6, bf16[2304,1152]{1,0:T(8,128)(2,1)S(1)} %bitcast.291), kind=kOutput, calls=%fused_computation.5 | convolution fusion | flops 5471207424 | bytes 17104896 | tf_op jit(solution)/shard_map/dot_general | solution.py:38
  219.2 4.7 fusion.28
  225.2 6.6 %fusion.30 = f32[512,1152]{1,0:T(8,128)S(1)} fusion(bf16[1152,2304]{1,0:T(8,128)(2,1)} %bitcast.316, bf16[1024,2304]{1,0:T(8,128)(2,1)} %copy-done.79), kind=kOutput, calls=%fused_computation.66 | convolution fusion | flops 2717908992 | bytes 10027008 | tf_op jit(solution)/shard_map/dot_general | solution.py:38
  231.9 3.6 fusion.17
  235.5 4.2 fusion.22
  240.4 2.5 collective-permute-done.21
  243.1 3.3 convolution_convert_fusion.2
  246.5 3.8 convolution_convert_fusion.1
  250.3 6.5 %multiply_convert_fusion = bf16[1024,2304]{1,0:T(8,128)(2,1)S(1)} fusion(bf16[1024,2304]{1,0:T(8,128)(2,1)S(1)} %bitcast.362, bf16[1024,1152]{1,0:T(8,128)(2,1)S(1)} %pad_maximum_fusion.7, bf16[1152,2304]{1,0:T(8,128)(2,1)S(1)} %bitcast.322), kind=kOutput, calls=%fused_computation.6 | convolution fusion | flops 5442895872 | bytes 17104896 | tf_op jit(solution)/shard_map/dot_general | solution.py:38
  256.9 6.7 %convolution_convert_fusion = bf16[2304,1152]{1,0:T(8,128)(2,1)S(1)} fusion(bf16[1024,2304]{1,0:T(8,128)(2,1)S(1)} %multiply_convert_fusion, bf16[1024,1152]{1,0:T(8,128)(2,1)S(1)} %copy-done.40), kind=kOutput, calls=%fused_computation.1 | convolution fusion | flops 5438472192 | bytes 12386304 | tf_op jit(solution)/shard_map/dot_general | solution.py:38
  263.6 5.0 pad_maximum_fusion.refs_1_
  268.6 7.8 %fusion.18 = f32[512,1152]{1,0:T(8,128)} fusion(bf16[2304,1152]{1,0:T(8,128)(2,1)} %shard_map.354, bf16[1024,2304]{1,0:T(8,128)(2,1)} %copy-done.80), kind=kOutput, calls=%fused_computation.40 | convolution fusion | flops 2717908992 | bytes 10027008 | tf_op jit(solution)/shard_map/dot_general | solution.py:38
  276.9 6.4 %fusion.20 = f32[512,1152]{1,0:T(8,128)S(1)} fusion(bf16[2304,1152]{1,0:T(8,128)(2,1)} %shard_map.354, bf16[1024,2304]{1,0:T(8,128)(2,1)} %copy-done.80), kind=kOutput, calls=%fused_computation.42 | convolution fusion | flops 2717908992 | bytes 10027008 | tf_op jit(solution)/shard_map/dot_general | solution.py:38
  283.3 2.9 fusion.92
  292.2 2.7 collective-permute-done.23
  295.1 3.2 fusion.39.refs_1_
  298.3 28.6 %shard_map.355 = bf16[1,1024,1728]{2,1,0:T(8,128)(2,1)} custom-call(bf16[1,1024,1728]{2,1,0:T(8,128)(2,1)} %fusion.9.refs_0_, bf16[1,1024,576]{2,1,0:T(8,128)(2,1)} %fusion.39.refs_1_, f32[1,1024,576]{2,1,0:T(8,128)} %copy-done.2, f32[1,8,1024]{2,1,0:T(8,128)} %copy-done.3), custom_call_target="tpu_custom_call" | custom-call | tf_op jit(solution)/shard_map/pallas_call | solution.py:370
  326.9 6.7 %convolution_convert_fusion.5 = bf16[1728,640]{1,0:T(8,128)(2,1)} fusion(bf16[1024,2,640]{0,2,1:T(8,128)(2,1)S(1)} %bitcast.336, s32[]{:T(128)S(6)} %select_n.309, bf16[1,1024,1728]{2,1,0:T(8,128)(2,1)} %shard_map.355), kind=kOutput, calls=%fused_computation.29 | convolution fusion | flops 2266030080 | bytes 7061508 | tf_op jit(solution)/shard_map/dot_general | solution.py:38
  333.7 4.3 convolution_convert_fusion.4
  338.1 3.1 convolution_convert_fusion.6
  347.1 5.3 %fusion.32 = f32[512,1280]{1,0:T(8,128)S(1)} fusion(bf16[1728,1280]{1,0:T(8,128)(2,1)} %bitcast.330, bf16[1024,1728]{1,0:T(8,128)(2,1)} %shard_map.356), kind=kOutput, calls=%fused_computation.75 | convolution fusion | flops 2264924160 | bytes 8880128 | tf_op jit(solution)/shard_map/dot_general | solution.py:38
  357.1 5.3 %fusion.34 = f32[512,1280]{1,0:T(8,128)S(1)} fusion(bf16[1728,1280]{1,0:T(8,128)(2,1)} %bitcast.331, bf16[1024,1728]{1,0:T(8,128)(2,1)} %shard_map.356), kind=kOutput, calls=%fused_computation.77 | convolution fusion | flops 2264924160 | bytes 8880128 | tf_op jit(solution)/shard_map/dot_general | solution.py:38
  362.5 2.1 add.362
  364.6 2.2 copy.200
  366.7 3.9 fusion.97
  370.6 2.3 copy.185
  381.5 3.9 add_add_fusion.2
  385.4 2.4 fusion.36.refs_0_
  390.8 4.2 all-to-all-start.1
  395.1 2.3 add_convert_fusion.2.refs_0_
  397.3 5.0 all-to-all-done.1
  405.8 3.8 all-to-all-start.2
  409.6 2.3 add_multiply_fusion
  411.9 19.4 %all-to-all-done.2 = f32[16,1,704]{2,1,0:T(1,128)S(1)} async-done(((f32[16,1,704]{2,1,0:T(1,128)}), f32[16,1,704]{2,1,0:T(1,128)S(1)}, u32[]{:S(2)}, u32[]{:S(2)}) %all-to-all-start.2) | async-done | bytes 45088 | tf_op jit(solution)/shard_map/all_to_all | solution.py:274
  431.9 2.7 fusion.38.refs_1_
  434.6 2.6 add_convert_fusion.1.refs_2_
  443.5 5.8 %collective-permute-done.34.refs_0_ = bf16[2,144,640]{2,1,0:T(8,128)(2,1)S(1)} collective-permute-done((bf16[2,144,640]{2,1,0:T(8,128)(2,1)S(1)}, bf16[2,144,640]{2,1,0:T(8,128)(2,1)S(1)}, u32[]{:S(2)}, u32[]{:S(2)}) %collective-permute-start.34) | collective-permute-done | bytes 368672 | tf_op jit(solution)/shard_map/ppermute | solution.py:90
  451.2 2.6 collective-permute-start.35
  453.8 7.2 %collective-permute-done.36.refs_0_ = bf16[2,144,640]{2,1,0:T(8,128)(2,1)S(1)} collective-permute-done((bf16[2,144,640]{2,1,0:T(8,128)(2,1)}, bf16[2,144,640]{2,1,0:T(8,128)(2,1)S(1)}, u32[]{:S(2)}, u32[]{:S(2)}) %collective-permute-start.36) | collective-permute-done | bytes 368672 | tf_op jit(solution)/shard_map/ppermute | solution.py:90
  463.0 19.8 %collective-permute-done.37 = bf16[1,144,640]{2,1,0:T(8,128)(2,1)S(1)} collective-permute-done((bf16[1,144,640]{2,1,0:T(8,128)(2,1)S(1)}, bf16[1,144,640]{2,1,0:T(8,128)(2,1)S(1)}, u32[]{:S(2)}, u32[]{:S(2)}) %collective-permute-start.37) | collective-permute-done | bytes 184352 | tf_op jit(solution)/shard_map/ppermute | solution.py:90
  482.9 2.4 add_multiply_fusion.3
  494.0 2.7 add_multiply_fusion.2
  (403 shorter events, 106.7 us)
Async XLA Ops:
  7.2 182.2 %all-gather.4.cloned.1.call-start = ((), (), s32[]{:S(2)}) async-start(), calls=%async_computation.5 | async-start | bytes 12847104 | tf_op jit(solution)/shard_map/all_gather | solution.py:463
  12.4 2.5 collective-permute-start.16
  14.7 1.5 collective-permute-start.17
  17.4 4.2 collective-permute-start
  17.6 22.2 %collective-permute-start.3 = (bf16[1,216,640]{2,1,0:T(8,128)(2,1)S(1)}, bf16[1,216,640]{2,1,0:T(8,128)(2,1)S(1)}, u32[]{:S(2)}, u32[]{:S(2)}) collective-permute-start(bf16[1,216,640]{2,1,0:T(8,128)(2,1)S(1)} %get-tuple-element.110), channel_id=1, source_target_pairs={{0,16},{2,18},{4,20},{6,22},{8,24},{10,26},{12,28},{14,30},{16,0},... | collective-permute-start | bytes 829448 | tf_op jit(solution)/shard_map/ppermute | solution.py:90
  21.7 3.7 collective-permute-start.1
  25.4 19.5 %collective-permute-start.2 = (bf16[2,2,1156]{2,1,0:T(2,128)(2,1)S(1)}, bf16[2,2,1156]{2,1,0:T(2,128)(2,1)S(1)}, u32[]{:S(2)}, u32[]{:S(2)}) collective-permute-start(bf16[2,2,1156]{2,1,0:T(2,128)(2,1)S(1)} %pad_maximum_fusion.20), channel_id=1, source_target_pairs={{0,4},{2,6},{4,0},{6,2},{8,12},{10,14},{12,8},{14,10},{16,20},{18,... | collective-permute-start | bytes 27752 | tf_op jit(solution)/shard_map/ppermute | solution.py:90
  40.0 22.5 %collective-permute-start.4 = (bf16[2,216,640]{2,1,0:T(8,128)(2,1)S(1)}, bf16[2,216,640]{2,1,0:T(8,128)(2,1)S(1)}, u32[]{:S(2)}, u32[]{:S(2)}) collective-permute-start(bf16[2,216,640]{2,1,0:T(8,128)(2,1)S(1)} %maximum_bitcast_fusion), channel_id=1, source_target_pairs={{0,8},{2,10},{4,12},{6,14},{8,0},{10,2},{12,4},{14,6},{16,24},{18,... | collective-permute-start | bytes 1658888 | tf_op jit(solution)/shard_map/ppermute | solution.py:90
  63.8 10.3 %copy-start.22 = (bf16[2,2,216,640]{3,2,1,0:T(8,128)(2,1)S(1)}, bf16[2,2,216,640]{3,2,1,0:T(8,128)(2,1)}, u32[]{:S(2)}) copy-start(bf16[2,2,216,640]{3,2,1,0:T(8,128)(2,1)} %copy.168) | copy-start | bytes 3317764
  63.8 4.8 collective-permute-start.5
  63.8 68.8 %copy-start.64 = (f32[512]{0:T(512)}, f32[512]{0:T(512)S(1)}, u32[]{:S(2)}) copy-start(f32[512]{0:T(512)S(1)} %broadcast_multiply_fusion.2) | copy-start | bytes 6148
  69.4 44.5 %copy-start.78 = (s32[2,4]{1,0:T(2,128)S(1)}, s32[2,4]{1,0:T(2,128)}, u32[]{:S(2)}) copy-start(s32[2,4]{1,0:T(2,128)} %constant.189.clone) | copy-start | bytes 100
  69.4 9.6 %collective-permute-start.6 = (bf16[8,2,1156]{2,1,0:T(2,128)(2,1)S(1)}, bf16[8,2,1156]{2,1,0:T(2,128)(2,1)S(1)}, u32[]{:S(2)}, u32[]{:S(2)}) collective-permute-start(bf16[8,2,1156]{2,1,0:T(2,128)(2,1)S(1)} %pad_maximum_fusion.18), channel_id=1, source_target_pairs={{0,16},{2,18},{4,20},{6,22},{8,24},{10,26},{12,28},{14,30},{16,0},... | collective-permute-start | bytes 110984 | tf_op jit(solution)/shard_map/ppermute | solution.py:90
  74.1 39.8 %copy-start.72 = (f32[512]{0:T(512)}, f32[512]{0:T(512)S(1)}, u32[]{:S(2)}) copy-start(f32[512]{0:T(512)S(1)} %fusion.15) | copy-start | bytes 6148
  74.2 23.2 %collective-permute-start.9 = (bf16[4,112,640]{2,1,0:T(8,128)(2,1)S(1)}, bf16[4,112,640]{2,1,0:T(8,128)(2,1)S(1)}, u32[]{:S(2)}, u32[]{:S(2)}) collective-permute-start(bf16[4,112,640]{2,1,0:T(8,128)(2,1)S(1)} %slice.106.refs_0_), channel_id=1, source_target_pairs={{0,2},{2,0},{4,6},{6,4},{8,10},{10,8},{12,14},{14,12},{16,18},{18,... | collective-permute-start | bytes 1720328 | tf_op jit(solution)/shard_map/ppermute | solution.py:90
  75.4 39.9 %collective-permute-start.10 = (bf16[4,112,640]{2,1,0:T(8,128)(2,1)S(1)}, bf16[4,112,640]{2,1,0:T(8,128)(2,1)S(1)}, u32[]{:S(2)}, u32[]{:S(2)}) collective-permute-start(bf16[4,112,640]{2,1,0:T(8,128)(2,1)S(1)} %slice.106.refs_0_), channel_id=1, source_target_pairs={{0,4},{2,6},{4,0},{6,2},{8,12},{10,14},{12,8},{14,10},{16,20},{18,... | collective-permute-start | bytes 1720328 | tf_op jit(solution)/shard_map/ppermute | solution.py:90
  77.1 29.3 %collective-permute-start.12 = (bf16[4,104,640]{2,1,0:T(8,128)(2,1)S(1)}, bf16[4,104,640]{2,1,0:T(8,128)(2,1)S(1)}, u32[]{:S(2)}, u32[]{:S(2)}) collective-permute-start(bf16[4,104,640]{2,1,0:T(8,128)(2,1)S(1)} %slice.107.refs_4_), channel_id=1, source_target_pairs={{0,4},{2,6},{4,0},{6,2},{8,12},{10,14},{12,8},{14,10},{16,20},{18,... | collective-permute-start | bytes 1597448 | tf_op jit(solution)/shard_map/ppermute | solution.py:90
  77.4 37.9 %collective-permute-start.13 = (bf16[4,104,640]{2,1,0:T(8,128)(2,1)S(1)}, bf16[4,104,640]{2,1,0:T(8,128)(2,1)}, u32[]{:S(2)}, u32[]{:S(2)}) collective-permute-start(bf16[4,104,640]{2,1,0:T(8,128)(2,1)S(1)} %slice.107.refs_4_), channel_id=1, source_target_pairs={{0,2},{2,0},{4,6},{6,4},{8,10},{10,8},{12,14},{14,12},{16,18},{18,... | collective-permute-start | bytes 1597448 | tf_op jit(solution)/shard_map/ppermute | solution.py:90
  79.3 20.0 %copy-start.58 = (f32[16,1,1152]{2,0,1:T(8,128)}, f32[16,1,1152]{2,0,1:T(8,128)S(1)}, u32[]{:S(2)}) copy-start(f32[16,1,1152]{2,0,1:T(8,128)S(1)} %copy.226) | copy-start | bytes 221188
  97.3 28.8 %collective-permute-start.11 = (bf16[4,112,640]{2,1,0:T(8,128)(2,1)S(1)}, bf16[4,112,640]{2,1,0:T(8,128)(2,1)S(1)}, u32[]{:S(2)}, u32[]{:S(2)}) collective-permute-start(bf16[4,112,640]{2,1,0:T(8,128)(2,1)S(1)} %collective-permute-done.9.refs_1_), channel_id=1, source_target_pairs={{0,4},{2,6},{4,0},{6,2},{8,12},{10,14},{12,8},{14,10},{16,20},{18,... | collective-permute-start | bytes 1720328 | tf_op jit(solution)/shard_map/ppermute | solution.py:90
  101.5 12.4 %all-to-all-start = ((f32[16,1,432]{2,1,0:T(1,128)}), f32[16,1,432]{2,1,0:T(1,128)S(1)}, u32[]{:S(2)}, u32[]{:S(2)}) async-start(f32[16,1,432]{2,1,0:T(1,128)} %copy.169), calls=%async_computation | async-start | bytes 65536 | tf_op jit(solution)/shard_map/all_to_all | solution.py:492
  106.3 379.8 %reduce-scatter.2.cloned.1.call-start = ((), (), s32[]{:S(2)}) async-start(), calls=%async_computation.4 | async-start | bytes 11280384 | tf_op jit(solution)/shard_map/reduce_scatter | solution.py:565
  106.4 19.8 %collective-permute-start.14 = (bf16[4,104,640]{2,1,0:T(8,128)(2,1)S(1)}, bf16[4,104,640]{2,1,0:T(8,128)(2,1)}, u32[]{:S(2)}, u32[]{:S(2)}) collective-permute-start(bf16[4,104,640]{2,1,0:T(8,128)(2,1)S(1)} %collective-permute-done.12.refs_5_), channel_id=1, source_target_pairs={{0,2},{2,0},{4,6},{6,4},{8,10},{10,8},{12,14},{14,12},{16,18},{18,... | collective-permute-start | bytes 1597448 | tf_op jit(solution)/shard_map/ppermute | solution.py:90
  108.4 24.3 %copy-start.67 = (f32[512]{0:T(512)}, f32[512]{0:T(512)S(1)}, u32[]{:S(2)}) copy-start(f32[512]{0:T(512)S(1)} %fusion.80) | copy-start | bytes 6148
  113.9 1.2 collective-permute-start.7
  132.6 9.2 %collective-permute-start.15 = (bf16[3,576,640]{2,1,0:T(8,128)(2,1)}, bf16[3,576,640]{2,1,0:T(8,128)(2,1)}, u32[]{:S(2)}, u32[]{:S(2)}) collective-permute-start(bf16[3,576,640]{2,1,0:T(8,128)(2,1)} %dynamic-slice_bitcast_fusion), channel_id=1, source_target_pairs={{0,1},{1,0},{2,3},{3,2},{4,5},{5,4},{6,7},{7,6},{8,9},{9,8},{10,11... | collective-permute-start | bytes 6635528 | tf_op jit(solution)/shard_map/ppermute | solution.py:58
  138.1 3.2 collective-permute-start.8
  193.8 4.6 collective-permute-start.18
  196.8 11.8 %copy-start.10 = (bf16[16,144,1152]{2,1,0:T(8,128)(2,1)}, bf16[16,144,1152]{2,1,0:T(8,128)(2,1)S(1)}, u32[]{:S(2)}) copy-start(bf16[16,144,1152]{2,1,0:T(8,128)(2,1)S(1)} %slice.108) | copy-start | bytes 15925252
  202.1 6.3 %collective-permute-start.19 = (bf16[512,1152]{1,0:T(8,128)(2,1)S(1)}, bf16[512,1152]{1,0:T(8,128)(2,1)S(1)}, u32[]{:S(2)}, u32[]{:S(2)}) collective-permute-start(bf16[512,1152]{1,0:T(8,128)(2,1)S(1)} %fusion.45), channel_id=1, source_target_pairs={{0,1},{1,0},{2,3},{3,2},{4,5},{5,4},{6,7},{7,6},{8,9},{9,8},{10,11... | collective-permute-start | bytes 3538952 | tf_op jit(solution)/shard_map/ppermute | solution.py:58
  208.4 10.8 %slice-start.2 = ((s8[5308416]{0:T(1024)(128)(4,1)}), s8[4194304]{0:T(1024)(128)(4,1)S(1)}, s32[]{:S(2)}) async-start(s8[5308416]{0:T(1024)(128)(4,1)} %bitcast.317), calls=%async_computation.8 | async-start | bytes 8388608
  208.6 10.6 %copy-start.39 = (bf16[1024,1152]{1,0:T(8,128)(2,1)}, bf16[1024,1152]{1,0:T(8,128)(2,1)S(1)}, u32[]{:S(2)}) copy-start(bf16[1024,1152]{1,0:T(8,128)(2,1)S(1)} %pad_maximum_fusion.6) | copy-start | bytes 7077892
  208.6 10.6 %slice-start.3 = ((s8[5308416]{0:T(1024)(128)(4,1)}), s8[1114112]{0:T(1024)(128)(4,1)S(1)}, s32[]{:S(2)}) async-start(s8[5308416]{0:T(1024)(128)(4,1)} %bitcast.317), calls=%async_computation.9 | async-start | bytes 2228224
  223.9 7.9 %collective-permute-start.20 = (f32[512,1152]{1,0:T(8,128)}, f32[512,1152]{1,0:T(8,128)}, u32[]{:S(2)}, u32[]{:S(2)}) collective-permute-start(f32[512,1152]{1,0:T(8,128)} %fusion.28), channel_id=1, source_target_pairs={{0,1},{1,0},{2,3},{3,2},{4,5},{5,4},{6,7},{7,6},{8,9},{9,8},{10,11... | collective-permute-start | bytes 7077896 | tf_op jit(solution)/shard_map/ppermute | solution.py:58
  231.9 11.2 %slice-start.6 = ((s8[4718592]{0:T(1024)(128)(4,1)}), s8[4194304]{0:T(1024)(128)(4,1)S(1)}, s32[]{:S(2)}) async-start(s8[4718592]{0:T(1024)(128)(4,1)} %bitcast.359), calls=%async_computation.12 | async-start | bytes 8388608
  239.9 3.0 collective-permute-start.21
  276.5 6.9 %collective-permute-start.22 = (f32[512,1152]{1,0:T(8,128)}, f32[512,1152]{1,0:T(8,128)}, u32[]{:S(2)}, u32[]{:S(2)}) collective-permute-start(f32[512,1152]{1,0:T(8,128)} %fusion.18), channel_id=1, source_target_pairs={{0,1},{1,0},{2,3},{3,2},{4,5},{5,4},{6,7},{7,6},{8,9},{9,8},{10,11... | collective-permute-start | bytes 7077896 | tf_op jit(solution)/shard_map/ppermute | solution.py:58
  292.0 2.9 collective-permute-start.23
  298.3 28.6 %copy-start.36 = (bf16[1024,1280]{0,1:T(8,128)(2,1)S(1)}, bf16[1024,1280]{0,1:T(8,128)(2,1)}, u32[]{:S(2)}) copy-start(bf16[1024,1280]{0,1:T(8,128)(2,1)} %copy-done.35) | copy-start | bytes 7864324
  333.6 7.6 %collective-permute-start.24 = (bf16[3,576,640]{2,1,0:T(8,128)(2,1)}, bf16[3,576,640]{2,1,0:T(8,128)(2,1)S(1)}, u32[]{:S(2)}, u32[]{:S(2)}) collective-permute-start(bf16[3,576,640]{2,1,0:T(8,128)(2,1)} %bitcast.54), channel_id=1, source_target_pairs={{0,1},{1,0},{2,3},{3,2},{4,5},{5,4},{6,7},{7,6},{8,9},{9,8},{10,11... | collective-permute-start | bytes 6635528 | tf_op jit(solution)/shard_map/ppermute | solution.py:58
  352.5 10.0 %collective-permute-start.25 = (f32[512,1280]{1,0:T(8,128)S(1)}, f32[512,1280]{1,0:T(8,128)}, u32[]{:S(2)}, u32[]{:S(2)}) collective-permute-start(f32[512,1280]{1,0:T(8,128)S(1)} %fusion.32), channel_id=1, source_target_pairs={{0,1},{1,0},{2,3},{3,2},{4,5},{5,4},{6,7},{7,6},{8,9},{9,8},{10,11... | collective-permute-start | bytes 7864328 | tf_op jit(solution)/shard_map/ppermute | solution.py:58
  353.1 34.8 %collective-permute-start.31 = (bf16[4,144,640]{2,1,0:T(8,128)(2,1)}, bf16[4,144,640]{2,1,0:T(8,128)(2,1)}, u32[]{:S(2)}, u32[]{:S(2)}) collective-permute-start(bf16[4,144,640]{2,1,0:T(8,128)(2,1)} %pad_maximum_fusion.13.refs_3_), channel_id=1, source_target_pairs={{0,4},{2,6},{4,0},{6,2},{8,12},{10,14},{12,8},{14,10},{16,20},{18,... | collective-permute-start | bytes 2211848 | tf_op jit(solution)/shard_map/ppermute | solution.py:90
  354.6 80.0 %collective-permute-start.30 = (bf16[4,144,640]{2,1,0:T(8,128)(2,1)}, bf16[4,144,640]{2,1,0:T(8,128)(2,1)}, u32[]{:S(2)}, u32[]{:S(2)}) collective-permute-start(bf16[4,144,640]{2,1,0:T(8,128)(2,1)} %pad_maximum_fusion.14.refs_4_), channel_id=1, source_target_pairs={{0,4},{2,6},{4,0},{6,2},{8,12},{10,14},{12,8},{14,10},{16,20},{18,... | collective-permute-start | bytes 2211848 | tf_op jit(solution)/shard_map/ppermute | solution.py:90
  355.1 25.7 %collective-permute-start.28 = (bf16[4,144,640]{2,1,0:T(8,128)(2,1)}, bf16[4,144,640]{2,1,0:T(8,128)(2,1)}, u32[]{:S(2)}, u32[]{:S(2)}) collective-permute-start(bf16[4,144,640]{2,1,0:T(8,128)(2,1)} %get-tuple-element.81.refs_1_), channel_id=1, source_target_pairs={{0,2},{2,0},{4,6},{6,4},{8,10},{10,8},{12,14},{14,12},{16,18},{18,... | collective-permute-start | bytes 2211848 | tf_op jit(solution)/shard_map/ppermute | solution.py:90
  356.1 75.8 %collective-permute-start.27 = (bf16[4,144,640]{2,1,0:T(8,128)(2,1)}, bf16[4,144,640]{2,1,0:T(8,128)(2,1)}, u32[]{:S(2)}, u32[]{:S(2)}) collective-permute-start(bf16[4,144,640]{2,1,0:T(8,128)(2,1)} %get-tuple-element.80.refs_2_), channel_id=1, source_target_pairs={{0,2},{2,0},{4,6},{6,4},{8,10},{10,8},{12,14},{14,12},{16,18},{18,... | collective-permute-start | bytes 2211848 | tf_op jit(solution)/shard_map/ppermute | solution.py:90
  380.8 7.1 %collective-permute-start.26 = (f32[1,6912]{1,0:T(1,128)}, f32[1,6912]{1,0:T(1,128)}, u32[]{:S(2)}, u32[]{:S(2)}) collective-permute-start(f32[1,6912]{1,0:T(1,128)} %constant_dynamic-update-slice_fusion.refs_1_), channel_id=1, source_target_pairs={{0,1},{1,0},{2,3},{3,2},{4,5},{5,4},{6,7},{7,6},{8,9},{9,8},{10,11... | collective-permute-start | bytes 82952 | tf_op jit(solution)/shard_map/ppermute | solution.py:58
  390.8 11.6 %all-to-all-start.1 = ((bf16[16,2,216]{2,1,0:T(2,128)(2,1)}), bf16[16,2,216]{2,1,0:T(2,128)(2,1)S(1)}, u32[]{:S(2)}, u32[]{:S(2)}) async-start(bf16[16,2,216]{2,1,0:T(2,128)(2,1)} %reshape.543), calls=%async_computation.1 | async-start | bytes 32768 | tf_op jit(solution)/shard_map/all_to_all | solution.py:620
  397.3 12.2 %copy-start.49 = (f32[576,432]{0,1:T(8,128)S(1)}, f32[576,432]{0,1:T(8,128)}, u32[]{:S(2)}) copy-start(f32[576,432]{0,1:T(8,128)} %param.36) | copy-start | bytes 2985988
  397.3 12.3 %copy-start.50 = (f32[576,432]{0,1:T(8,128)S(1)}, f32[576,432]{0,1:T(8,128)}, u32[]{:S(2)}) copy-start(f32[576,432]{0,1:T(8,128)} %param.31) | copy-start | bytes 2985988
  397.3 12.3 %copy-start.59 = (f32[16,1,1152]{2,0,1:T(8,128)S(1)}, f32[16,1,1152]{2,0,1:T(8,128)}, u32[]{:S(2)}) copy-start(f32[16,1,1152]{2,0,1:T(8,128)} %copy-done.58) | copy-start | bytes 221188
  403.1 31.5 %collective-permute-start.32 = (bf16[4,144,640]{2,1,0:T(8,128)(2,1)}, bf16[4,144,640]{2,1,0:T(8,128)(2,1)}, u32[]{:S(2)}, u32[]{:S(2)}) collective-permute-start(bf16[4,144,640]{2,1,0:T(8,128)(2,1)} %shard_map.360), channel_id=1, source_target_pairs={{0,2},{2,0},{4,6},{6,4},{8,10},{10,8},{12,14},{14,12},{16,18},{18,... | collective-permute-start | bytes 2211848 | tf_op jit(solution)/shard_map/ppermute | solution.py:90
  403.7 28.2 %collective-permute-start.29 = (bf16[4,144,640]{2,1,0:T(8,128)(2,1)}, bf16[4,144,640]{2,1,0:T(8,128)(2,1)}, u32[]{:S(2)}, u32[]{:S(2)}) collective-permute-start(bf16[4,144,640]{2,1,0:T(8,128)(2,1)} %shard_map.358), channel_id=1, source_target_pairs={{0,4},{2,6},{4,0},{6,2},{8,12},{10,14},{12,8},{14,10},{16,20},{18,... | collective-permute-start | bytes 2211848 | tf_op jit(solution)/shard_map/ppermute | solution.py:90
  405.8 25.5 %all-to-all-start.2 = ((f32[16,1,704]{2,1,0:T(1,128)}), f32[16,1,704]{2,1,0:T(1,128)S(1)}, u32[]{:S(2)}, u32[]{:S(2)}) async-start(f32[16,1,704]{2,1,0:T(1,128)} %copy.187), calls=%async_computation.2 | async-start | bytes 98304 | tf_op jit(solution)/shard_map/all_to_all | solution.py:274
  411.9 22.7 %copy-start.42 = (bf16[4,72,640]{2,1,0:T(8,128)(2,1)S(1)}, bf16[4,72,640]{2,1,0:T(8,128)(2,1)}, u32[]{:S(2)}) copy-start(bf16[4,72,640]{2,1,0:T(8,128)(2,1)} %get-tuple-element.88) | copy-start | bytes 1105924
  411.9 22.7 %copy-start.43 = (bf16[4,72,640]{2,1,0:T(8,128)(2,1)S(1)}, bf16[4,72,640]{2,1,0:T(8,128)(2,1)}, u32[]{:S(2)}) copy-start(bf16[4,72,640]{2,1,0:T(8,128)(2,1)} %get-tuple-element.129) | copy-start | bytes 1105924
  437.2 2.9 collective-permute-start.33
  437.2 12.0 %collective-permute-start.34 = (bf16[2,144,640]{2,1,0:T(8,128)(2,1)S(1)}, bf16[2,144,640]{2,1,0:T(8,128)(2,1)S(1)}, u32[]{:S(2)}, u32[]{:S(2)}) collective-permute-start(bf16[2,144,640]{2,1,0:T(8,128)(2,1)S(1)} %dynamic-slice_bitcast_fusion.4), channel_id=1, source_target_pairs={{0,8},{2,10},{4,12},{6,14},{8,0},{10,2},{12,4},{14,6},{16,24},{18,... | collective-permute-start | bytes 1105928 | tf_op jit(solution)/shard_map/ppermute | solution.py:90
  439.1 21.9 %collective-permute-start.36 = (bf16[2,144,640]{2,1,0:T(8,128)(2,1)}, bf16[2,144,640]{2,1,0:T(8,128)(2,1)S(1)}, u32[]{:S(2)}, u32[]{:S(2)}) collective-permute-start(bf16[2,144,640]{2,1,0:T(8,128)(2,1)} %dynamic-slice_bitcast_fusion.3), channel_id=1, source_target_pairs={{0,8},{2,10},{4,12},{6,14},{8,0},{10,2},{12,4},{14,6},{16,24},{18,... | collective-permute-start | bytes 1105928 | tf_op jit(solution)/shard_map/ppermute | solution.py:90
  450.0 32.9 %copy-start.41 = (f32[576,216]{0,1:T(8,128)S(1)}, f32[576,216]{0,1:T(8,128)}, u32[]{:S(2)}) copy-start(f32[576,216]{0,1:T(8,128)} %param.27) | copy-start | bytes 1492996
  450.0 32.9 %copy-start.56 = (f32[576,216]{0,1:T(8,128)S(1)}, f32[576,216]{0,1:T(8,128)}, u32[]{:S(2)}) copy-start(f32[576,216]{0,1:T(8,128)} %param.37) | copy-start | bytes 1492996
  451.2 11.8 %collective-permute-start.35 = (bf16[1,144,640]{2,1,0:T(8,128)(2,1)S(1)}, bf16[1,144,640]{2,1,0:T(8,128)(2,1)S(1)}, u32[]{:S(2)}, u32[]{:S(2)}) collective-permute-start(bf16[1,144,640]{2,1,0:T(8,128)(2,1)S(1)} %constant_dynamic-slice_fusion.3), channel_id=1, source_target_pairs={{0,16},{2,18},{4,20},{6,22},{8,24},{10,26},{12,28},{14,30},{16,0},... | collective-permute-start | bytes 552968 | tf_op jit(solution)/shard_map/ppermute | solution.py:90
  462.9 20.0 %collective-permute-start.37 = (bf16[1,144,640]{2,1,0:T(8,128)(2,1)S(1)}, bf16[1,144,640]{2,1,0:T(8,128)(2,1)S(1)}, u32[]{:S(2)}, u32[]{:S(2)}) collective-permute-start(bf16[1,144,640]{2,1,0:T(8,128)(2,1)S(1)} %constant_dynamic-slice_fusion.2), channel_id=1, source_target_pairs={{0,16},{2,18},{4,20},{6,22},{8,24},{10,26},{12,28},{14,30},{16,0},... | collective-permute-start | bytes 552968 | tf_op jit(solution)/shard_map/ppermute | solution.py:90
  487.3 3.3 collective-permute-start.39
  490.1 6.6 %collective-permute-start.38 = (bf16[144,576]{1,0:T(8,128)(2,1)}, bf16[144,576]{1,0:T(8,128)(2,1)}, u32[]{:S(2)}, u32[]{:S(2)}) collective-permute-start(bf16[144,576]{1,0:T(8,128)(2,1)} %bitcast.280), channel_id=1, source_target_pairs={{0,1},{1,0},{2,3},{3,2},{4,5},{5,4},{6,7},{7,6},{8,9},{9,8},{10,11... | collective-permute-start | bytes 497672 | tf_op jit(solution)/shard_map/ppermute | solution.py:58
  (72 other events, 284.4 us)
Sparse Core Ops, SparseCore 0:
  17.4 171.9 all-gather.3
  277.0 209.1 reduce-scatter.1
where the time goes:
time: 517 us; the launch traced here: 507 us
  waiting for transfers between devices  150 us (29%)
  matrix products  97.5 us (19%)
  other arithmetic  79.3 us (15%)
  local copies, waits for them, and re-layouts  58.1 us (11%)
  Pallas kernels  53.3 us (10%)
  starting transfers between devices  51.2 us (10%)
  between operations  18.3 us (4%)
    ppermute x22, waiting for transfers between devices, swap(): return lax.ppermute(array, 'dp', [(j, j ^ bit) for j in range(size)])  98.9 us
    dot_general x21, matrix products, dot(): lax.dot_general(first, second, (over, ((), ())), preferred_element_type=j...  97.5 us
    ppermute x22, starting transfers between devices, swap(): return lax.ppermute(array, 'dp', [(j, j ^ bit) for j in range(size)])  33.8 us
    pallas_call x1, Pallas kernels, attend_back(): pl.pallas_call(lambda *refs: softmax_back_kernel(heads, head_size, math.g...  28.6 us
    pallas_call x1, Pallas kernels, attend(): pl.pallas_call(lambda *refs: softmax_kernel(heads, head_size, math.gcd(le...  22.3 us
    unnamed x192, local copies, waits for them, and re-layouts  20.3 us
    all_to_all x1, waiting for transfers between devices, sum_small(): return jnp.sum(lax.all_to_all(blocks, 'dp', 0, 0, tiled=True), axis=0)  19.4 us
    convert_element_type x6, other arithmetic, plus(): sum((part.astype(jnp.float32) for part in parts)).astype(parts[0].dtype)  12.2 us
  transfers between devices with their start and end apart: 45, of which 21 were waited for; matrix products, arithmetic and copies ran while one was open for 29% of the time, Pallas kernels for 11%

commit v1 on v0

--- a/solution.py
+++ b/solution.py
@@ -250,6 +250,28 @@
             held = plus(lax.dynamic_index_in_dim(pairs, mine, 1, False), came(swap(away, bit)))
             bit <<= 1
         return held[0]
+
+
+def by_low(blocks):
+    if not hypercube():
+        return blocks
+    return jnp.swapaxes(blocks.reshape((-1, 4) + blocks.shape[1:]), 0, 1)
+
+
+def sum_low(blocks):
+    if not hypercube():
+        return blocks
+    size = lax.axis_size("dp")
+    groups = [[n + m for m in range(4)] for n in range(0, size, 4)]
+    return lax.psum_scatter(blocks, "dp", axis_index_groups=groups, tiled=False)
+
+
+def sum_high(blocks):
+    if not hypercube():
+        return lax.psum_scatter(blocks, "dp", tiled=False)
+    size = lax.axis_size("dp")
+    groups = [list(range(m, size, 4)) for m in range(4)]
+    return lax.psum_scatter(blocks, "dp", axis_index_groups=groups, tiled=False)
 
 
 def gather_small(own, *others):
@@ -560,15 +582,9 @@
     expansion_grad = expansion_grad.reshape(dp_size, hidden_piece, width)
     if contraction_grad[0].shape[-1] != width:
         contraction_grad = [widen_blocks(part) for part in contraction_grad]
-    mlp_grads = jnp.concatenate(contraction_grad + [expansion_grad], axis=1)
+    mlp_grads = by_low(jnp.concatenate(contraction_grad + [expansion_grad], axis=1))
     expansion_back = after(expansion_full, mlp_grads)
-    mlp_sum = lax.psum_scatter(mlp_grads, "dp", scatter_dimension=0, tiled=False)
-    if cut_c == seq_size * proj_share:
-        contraction_sum = by_distance(mlp_sum[:cut_c].reshape(seq_size, proj_share, width), 0)
-    else:
-        contraction_sum = narrow(mlp_sum[:cut_c], proj_share).reshape(proj_share, seq_size, -1)
-        contraction_sum = by_distance(contraction_sum, 1)
-    expansion_sum = mlp_sum[cut_c:]
+    mlp_sum = sum_low(mlp_grads)
     mlp_input_grad = own_shape(
         sum_tokens([nn(rows, expansion_back) for rows in by_block(hidden_pre_grad)])
     )
@@ -635,6 +651,13 @@
     silu_pull = jax.vjp(silu_of, condition.astype(jnp.float32))[1]
     condition_grad = silu_pull(cond_grad)[0]
 
+    mlp_sum = sum_high(after(mlp_sum, mod_grad))
+    if cut_c == seq_size * proj_share:
+        contraction_sum = by_distance(mlp_sum[:cut_c].reshape(seq_size, proj_share, width), 0)
+    else:
+        contraction_sum = narrow(mlp_sum[:cut_c], proj_share).reshape(proj_share, seq_size, -1)
+        contraction_sum = by_distance(contraction_sum, 1)
+    expansion_sum = mlp_sum[cut_c:]
     waits = ([back],)
     attention_sum = jnp.concatenate([part.finish(*waits) for part in attention_sum], axis=0)
     expansion_sum = around(

time: 517 us -> 511 us (0.988)
  other arithmetic: 79.3 us -> 73.2 us
  starting transfers between devices: 51.2 us -> 57.3 us
  matrix products: 97.5 us -> 92 us
    ppermute x22, waiting for transfers between devices: 98.9 us -> 114 us  [swap(): return lax.ppermute(array, 'dp', [(j, j ^ bit) for j in range(size)])]
    all_to_all x1, waiting for transfers between devices: 19.4 us -> 8.16 us  [sum_small(): return jnp.sum(lax.all_to_all(blocks, 'dp', 0, 0, tiled=True), axis=0)]
    dot_general x21, matrix products: 97.5 us -> 92 us  [dot(): lax.dot_general(first, second, (over, ((), ())), preferred_element_type=j...]
    unnamed x192 -> x210, local copies, waits for them, and re-layouts: 20.3 us -> 20 us
  transfers between devices with their start and end apart: 45 -> 46, of which waited for: 21 -> 24; matrix products, arithmetic and copies ran while one was open for 29% -> 29% of each run, Pallas kernels for 11% -> 11%
where the time goes in v1:
time: 511 us; the launch traced here: 502 us
  waiting for transfers between devices  150 us (29%)
  matrix products  92 us (18%)
  other arithmetic  73.2 us (14%)
  local copies, waits for them, and re-layouts  58.1 us (11%)
  starting transfers between devices  57.3 us (11%)
  Pallas kernels  53.2 us (10%)
  between operations  18.1 us (4%)
    ppermute x22, waiting for transfers between devices, swap(): return lax.ppermute(array, 'dp', [(j, j ^ bit) for j in range(size)])  114 us
    dot_general x21, matrix products, dot(): lax.dot_general(first, second, (over, ((), ())), preferred_element_type=j...  92 us
    ppermute x22, starting transfers between devices, swap(): return lax.ppermute(array, 'dp', [(j, j ^ bit) for j in range(size)])  35.8 us
    pallas_call x1, Pallas kernels, attend_back(): pl.pallas_call(lambda *refs: softmax_back_kernel(heads, head_size, math.g...  28.5 us
    pallas_call x1, Pallas kernels, attend(): pl.pallas_call(lambda *refs: softmax_kernel(heads, head_size, math.gcd(le...  22.3 us
    unnamed x210, local copies, waits for them, and re-layouts  20 us
    convert_element_type x6, other arithmetic, plus(): sum((part.astype(jnp.float32) for part in parts)).astype(parts[0].dtype)  12.4 us
    ppermute x18, waiting for transfers between devices, around(): got[(size - r) % size] = lax.ppermute(pieces[r], 'seq', steps)  11.4 us
  transfers between devices with their start and end apart: 46, of which 24 were waited for; matrix products, arithmetic and copies ran while one was open for 29% of the time, Pallas kernels for 11%

profile of v1, /device:TPU:0, one launch (start us, length us, event | category | flops | bytes accessed | tf_op | source)
XLA Modules:
  0.0 501.7 jit_solution(13096672151634317662)
XLA Ops:
  17.6 4.0 collective-permute-start.3
  27.0 12.8 %collective-permute-done.3 = bf16[1,216,640]{2,1,0:T(8,128)(2,1)S(1)} collective-permute-done((bf16[1,216,640]{2,1,0:T(8,128)(2,1)S(1)}, bf16[1,216,640]{2,1,0:T(8,128)(2,1)S(1)}, u32[]{:S(2)}, u32[]{:S(2)}) %collective-permute-start.3) | collective-permute-done | bytes 276512 | tf_op jit(solution)/shard_map/ppermute | solution.py:90
  40.0 4.9 collective-permute-start.4
  45.5 17.0 %collective-permute-done.4 = bf16[2,216,640]{2,1,0:T(8,128)(2,1)S(1)} collective-permute-done((bf16[2,216,640]{2,1,0:T(8,128)(2,1)S(1)}, bf16[2,216,640]{2,1,0:T(8,128)(2,1)S(1)}, u32[]{:S(2)}, u32[]{:S(2)}) %collective-permute-start.4) | collective-permute-done | bytes 552992 | tf_op jit(solution)/shard_map/ppermute | solution.py:90
  63.8 4.7 collective-permute-done.5
  69.4 4.2 collective-permute-start.6
  79.3 18.1 %collective-permute-done.9.refs_1_ = bf16[4,112,640]{2,1,0:T(8,128)(2,1)S(1)} collective-permute-done((bf16[4,112,640]{2,1,0:T(8,128)(2,1)S(1)}, bf16[4,112,640]{2,1,0:T(8,128)(2,1)S(1)}, u32[]{:S(2)}, u32[]{:S(2)}) %collective-permute-start.9) | collective-permute-done | bytes 573472 | tf_op jit(solution)/shard_map/ppermute | solution.py:90
  101.5 4.9 all-to-all-start
  106.4 2.0 collective-permute-start.14
  108.4 5.4 %all-to-all-done = f32[16,1,432]{2,1,0:T(1,128)S(1)} async-done(((f32[16,1,432]{2,1,0:T(1,128)}), f32[16,1,432]{2,1,0:T(1,128)S(1)}, u32[]{:S(2)}, u32[]{:S(2)}) %all-to-all-start) | async-done | bytes 27680 | tf_op jit(solution)/shard_map/all_to_all | solution.py:514
  115.3 10.9 %collective-permute-done.14.refs_7_ = bf16[4,104,640]{2,1,0:T(8,128)(2,1)} collective-permute-done((bf16[4,104,640]{2,1,0:T(8,128)(2,1)S(1)}, bf16[4,104,640]{2,1,0:T(8,128)(2,1)}, u32[]{:S(2)}, u32[]{:S(2)}) %collective-permute-start.14) | collective-permute-done | bytes 532512 | tf_op jit(solution)/shard_map/ppermute | solution.py:90
  126.2 2.4 shard_map.349
  129.0 2.0 copy-done.18
  134.1 2.4 copy.183
  138.6 2.7 collective-permute-done.8
  141.7 3.0 bitcast_select_fusion.1
  145.1 2.1 copy-done.33
  147.2 6.6 %fusion.9.refs_0_ = bf16[1,1024,1728]{2,1,0:T(8,128)(2,1)} fusion(bf16[1024,1280]{0,1:T(8,128)(2,1)S(1)} %pad_maximum_fusion.5, bf16[1728,1280]{1,0:T(8,128)(2,1)S(1)} %bitcast.334), kind=kOutput, calls=%fused_computation.28 | convolution fusion | flops 4531617792 | bytes 10584064 | tf_op jit(solution)/shard_map/dot_general | solution.py:38
  153.8 22.3 %shard_map.350 = (f32[1,1024,576]{2,1,0:T(8,128)S(1)}, bf16[1,1024,576]{2,1,0:T(8,128)(2,1)S(1)}, f32[1,8,1024]{2,1,0:T(8,128)S(1)}) custom-call(bf16[1,1024,1728]{2,1,0:T(8,128)(2,1)} %fusion.9.refs_0_), custom_call_target="tpu_custom_call" | custom-call | flops 2415919104 | bytes 83886080 | tf_op jit(solution)/shard_map/pallas_call | solution.py:324
  179.3 10.1 %all-gather.4.cloned.1.call-done.refs_0_ = bf16[16,324,1152]{2,1,0:T(8,128)(2,1)} async-done(((bf16[1,324,1152]{2,1,0:T(8,128)(2,1)}), bf16[16,324,1152]{2,1,0:T(8,128)(2,1)}) %all-gather.4.cloned.1.call-update) | async-done | bytes 11943952 | tf_op jit(solution)/shard_map/all_gather | solution.py:485
  193.9 2.9 slice.108
  202.5 3.0 fusion.95
  205.5 2.9 pad_maximum_fusion.1
  208.7 10.6 %fusion.2 = (bf16[1024,2304]{1,0:T(8,128)(2,1)}, bf16[1024,2304]{1,0:T(8,128)(2,1)S(1)}) fusion(bf16[1024,1152]{1,0:T(8,128)(2,1)S(1)} %pad_maximum_fusion.6, bf16[2304,1152]{1,0:T(8,128)(2,1)S(1)} %bitcast.295), kind=kOutput, calls=%fused_computation.6 | convolution fusion | flops 5471207424 | bytes 17104896 | tf_op jit(solution)/shard_map/dot_general | solution.py:38
  219.3 4.7 fusion.28
  225.2 6.6 %fusion.30 = f32[512,1152]{1,0:T(8,128)S(1)} fusion(bf16[1152,2304]{1,0:T(8,128)(2,1)} %bitcast.321, bf16[1024,2304]{1,0:T(8,128)(2,1)} %copy-done.86), kind=kOutput, calls=%fused_computation.67 | convolution fusion | flops 2717908992 | bytes 10027008 | tf_op jit(solution)/shard_map/dot_general | solution.py:38
  231.9 3.6 fusion.17
  235.5 4.2 fusion.22
  240.4 2.5 collective-permute-done.21
  243.1 3.3 convolution_convert_fusion.2
  246.5 3.8 convolution_convert_fusion.1
  250.4 6.5 %multiply_convert_fusion = bf16[1024,2304]{1,0:T(8,128)(2,1)S(1)} fusion(bf16[1024,2304]{1,0:T(8,128)(2,1)S(1)} %bitcast.370, bf16[1024,1152]{1,0:T(8,128)(2,1)S(1)} %pad_maximum_fusion.7, bf16[1152,2304]{1,0:T(8,128)(2,1)S(1)} %bitcast.327), kind=kOutput, calls=%fused_computation.7 | convolution fusion | flops 5442895872 | bytes 17104896 | tf_op jit(solution)/shard_map/dot_general | solution.py:38
  256.9 6.7 %convolution_convert_fusion = bf16[2304,1152]{1,0:T(8,128)(2,1)S(1)} fusion(bf16[1024,2304]{1,0:T(8,128)(2,1)S(1)} %multiply_convert_fusion, bf16[1024,1152]{1,0:T(8,128)(2,1)S(1)} %copy-done.43), kind=kOutput, calls=%fused_computation.1 | convolution fusion | flops 5438472192 | bytes 12386304 | tf_op jit(solution)/shard_map/dot_general | solution.py:38
  263.6 5.0 copy_bitcast_fusion.refs_1_
  268.7 6.6 %fusion.18 = f32[512,1152]{1,0:T(8,128)S(1)} fusion(bf16[2304,1152]{1,0:T(8,128)(2,1)} %shard_map.354, bf16[1024,2304]{1,0:T(8,128)(2,1)} %copy-done.87), kind=kOutput, calls=%fused_computation.41 | convolution fusion | flops 2717908992 | bytes 10027008 | tf_op jit(solution)/shard_map/dot_general | solution.py:38
  275.7 4.9 fusion.20
  288.5 2.8 collective-permute-done.23
  291.5 3.2 fusion.39.refs_1_
  294.8 28.5 %shard_map.355 = bf16[1,1024,1728]{2,1,0:T(8,128)(2,1)} custom-call(bf16[1,1024,1728]{2,1,0:T(8,128)(2,1)} %fusion.9.refs_0_, bf16[1,1024,576]{2,1,0:T(8,128)(2,1)} %fusion.39.refs_1_, f32[1,1024,576]{2,1,0:T(8,128)} %copy-done.2, f32[1,8,1024]{2,1,0:T(8,128)} %copy-done.3), custom_call_target="tpu_custom_call" | custom-call | tf_op jit(solution)/shard_map/pallas_call | solution.py:392
  323.3 6.5 %convolution_convert_fusion.5 = bf16[1728,640]{1,0:T(8,128)(2,1)} fusion(bf16[1024,2,640]{0,2,1:T(8,128)(2,1)S(1)} %bitcast.343, s32[]{:T(128)S(6)} %select_n.309, bf16[1,1024,1728]{2,1,0:T(8,128)(2,1)} %shard_map.355), kind=kOutput, calls=%fused_computation.30 | convolution fusion | flops 2266030080 | bytes 7061508 | tf_op jit(solution)/shard_map/dot_general | solution.py:38
  329.8 4.4 convolution_convert_fusion.4
  334.2 3.1 convolution_convert_fusion.6
  343.3 5.5 %fusion.32 = f32[512,1280]{1,0:T(8,128)S(1)} fusion(bf16[1728,1280]{1,0:T(8,128)(2,1)} %bitcast.335, bf16[1024,1728]{1,0:T(8,128)(2,1)} %shard_map.356), kind=kOutput, calls=%fused_computation.76 | convolution fusion | flops 2264924160 | bytes 8880128 | tf_op jit(solution)/shard_map/dot_general | solution.py:38
  351.4 2.5 fusion.34
  354.3 2.1 copy.217
  356.4 3.8 fusion.97
  360.3 2.5 copy.201
  371.9 4.6 all-to-all-start.1
  376.6 2.0 collective-permute-start.30
  380.0 4.9 collective-permute-done.31.refs_0_
  390.0 2.5 fusion.36.refs_0_
  392.5 2.4 add_convert_fusion.2.refs_0_
  394.9 2.2 add_add_fusion.2
  397.1 2.0 collective-permute-start.32
  400.7 7.7 %all-to-all-start.2 = ((f32[16,1,704]{2,1,0:T(1,128)}), f32[16,1,704]{2,1,0:T(1,128)S(1)}, u32[]{:S(2)}, u32[]{:S(2)}) async-start(f32[16,1,704]{2,1,0:T(1,128)} %copy.203), calls=%async_computation.2 | async-start | bytes 98304 | tf_op jit(solution)/shard_map/all_to_all | solution.py:296
  408.5 2.3 add_multiply_fusion
  410.8 8.2 %all-to-all-done.2 = f32[16,1,704]{2,1,0:T(1,128)S(1)} async-done(((f32[16,1,704]{2,1,0:T(1,128)}), f32[16,1,704]{2,1,0:T(1,128)S(1)}, u32[]{:S(2)}, u32[]{:S(2)}) %all-to-all-start.2) | async-done | bytes 45088 | tf_op jit(solution)/shard_map/all_to_all | solution.py:296
  419.6 2.7 fusion.38.refs_1_
  422.3 2.6 add_convert_fusion.1.refs_2_
  431.6 17.9 %collective-permute-done.34.refs_0_ = bf16[2,144,640]{2,1,0:T(8,128)(2,1)S(1)} collective-permute-done((bf16[2,144,640]{2,1,0:T(8,128)(2,1)S(1)}, bf16[2,144,640]{2,1,0:T(8,128)(2,1)S(1)}, u32[]{:S(2)}, u32[]{:S(2)}) %collective-permute-start.34) | collective-permute-done | bytes 368672 | tf_op jit(solution)/shard_map/ppermute | solution.py:90
  452.1 12.8 %collective-permute-done.36.refs_0_ = bf16[2,144,640]{2,1,0:T(8,128)(2,1)S(1)} collective-permute-done((bf16[2,144,640]{2,1,0:T(8,128)(2,1)}, bf16[2,144,640]{2,1,0:T(8,128)(2,1)S(1)}, u32[]{:S(2)}, u32[]{:S(2)}) %collective-permute-start.36) | collective-permute-done | bytes 368672 | tf_op jit(solution)/shard_map/ppermute | solution.py:90
  467.7 10.5 %collective-permute-done.37 = bf16[1,144,640]{2,1,0:T(8,128)(2,1)S(1)} collective-permute-done((bf16[1,144,640]{2,1,0:T(8,128)(2,1)S(1)}, bf16[1,144,640]{2,1,0:T(8,128)(2,1)S(1)}, u32[]{:S(2)}, u32[]{:S(2)}) %collective-permute-start.37) | collective-permute-done | bytes 184352 | tf_op jit(solution)/shard_map/ppermute | solution.py:90
  478.3 2.4 add_multiply_fusion.3
  488.6 2.7 add_multiply_fusion.2
  (426 shorter events, 108.1 us)
Async XLA Ops:
  7.2 182.2 %all-gather.4.cloned.1.call-start = ((), (), s32[]{:S(2)}) async-start(), calls=%async_computation.6 | async-start | bytes 12847104 | tf_op jit(solution)/shard_map/all_gather | solution.py:485
  12.4 2.5 collective-permute-start.16
  14.7 1.5 collective-permute-start.17
  17.4 4.2 collective-permute-start
  17.6 22.2 %collective-permute-start.3 = (bf16[1,216,640]{2,1,0:T(8,128)(2,1)S(1)}, bf16[1,216,640]{2,1,0:T(8,128)(2,1)S(1)}, u32[]{:S(2)}, u32[]{:S(2)}) collective-permute-start(bf16[1,216,640]{2,1,0:T(8,128)(2,1)S(1)} %get-tuple-element.110), channel_id=1, source_target_pairs={{0,16},{2,18},{4,20},{6,22},{8,24},{10,26},{12,28},{14,30},{16,0},... | collective-permute-start | bytes 829448 | tf_op jit(solution)/shard_map/ppermute | solution.py:90
  21.7 3.7 collective-permute-start.1
  25.4 19.5 %collective-permute-start.2 = (bf16[2,2,1156]{2,1,0:T(2,128)(2,1)S(1)}, bf16[2,2,1156]{2,1,0:T(2,128)(2,1)S(1)}, u32[]{:S(2)}, u32[]{:S(2)}) collective-permute-start(bf16[2,2,1156]{2,1,0:T(2,128)(2,1)S(1)} %pad_maximum_fusion.20), channel_id=1, source_target_pairs={{0,4},{2,6},{4,0},{6,2},{8,12},{10,14},{12,8},{14,10},{16,20},{18,... | collective-permute-start | bytes 27752 | tf_op jit(solution)/shard_map/ppermute | solution.py:90
  40.0 22.5 %collective-permute-start.4 = (bf16[2,216,640]{2,1,0:T(8,128)(2,1)S(1)}, bf16[2,216,640]{2,1,0:T(8,128)(2,1)S(1)}, u32[]{:S(2)}, u32[]{:S(2)}) collective-permute-start(bf16[2,216,640]{2,1,0:T(8,128)(2,1)S(1)} %maximum_bitcast_fusion), channel_id=1, source_target_pairs={{0,8},{2,10},{4,12},{6,14},{8,0},{10,2},{12,4},{14,6},{16,24},{18,... | collective-permute-start | bytes 1658888 | tf_op jit(solution)/shard_map/ppermute | solution.py:90
  63.8 4.8 collective-permute-start.5
  63.8 68.8 %copy-start.67 = (f32[512]{0:T(512)}, f32[512]{0:T(512)S(1)}, u32[]{:S(2)}) copy-start(f32[512]{0:T(512)S(1)} %broadcast_multiply_fusion.2) | copy-start | bytes 6148
  69.4 44.5 %copy-start.85 = (s32[2,4]{1,0:T(2,128)S(1)}, s32[2,4]{1,0:T(2,128)}, u32[]{:S(2)}) copy-start(s32[2,4]{1,0:T(2,128)} %constant.189.clone) | copy-start | bytes 100
  69.4 9.6 %collective-permute-start.6 = (bf16[8,2,1156]{2,1,0:T(2,128)(2,1)S(1)}, bf16[8,2,1156]{2,1,0:T(2,128)(2,1)S(1)}, u32[]{:S(2)}, u32[]{:S(2)}) collective-permute-start(bf16[8,2,1156]{2,1,0:T(2,128)(2,1)S(1)} %pad_maximum_fusion.18), channel_id=1, source_target_pairs={{0,16},{2,18},{4,20},{6,22},{8,24},{10,26},{12,28},{14,30},{16,0},... | collective-permute-start | bytes 110984 | tf_op jit(solution)/shard_map/ppermute | solution.py:90
  74.1 39.8 %copy-start.77 = (f32[512]{0:T(512)}, f32[512]{0:T(512)S(1)}, u32[]{:S(2)}) copy-start(f32[512]{0:T(512)S(1)} %fusion.15) | copy-start | bytes 6148
  74.2 23.2 %collective-permute-start.9 = (bf16[4,112,640]{2,1,0:T(8,128)(2,1)S(1)}, bf16[4,112,640]{2,1,0:T(8,128)(2,1)S(1)}, u32[]{:S(2)}, u32[]{:S(2)}) collective-permute-start(bf16[4,112,640]{2,1,0:T(8,128)(2,1)S(1)} %slice.106.refs_0_), channel_id=1, source_target_pairs={{0,2},{2,0},{4,6},{6,4},{8,10},{10,8},{12,14},{14,12},{16,18},{18,... | collective-permute-start | bytes 1720328 | tf_op jit(solution)/shard_map/ppermute | solution.py:90
  75.4 39.9 %collective-permute-start.10 = (bf16[4,112,640]{2,1,0:T(8,128)(2,1)S(1)}, bf16[4,112,640]{2,1,0:T(8,128)(2,1)S(1)}, u32[]{:S(2)}, u32[]{:S(2)}) collective-permute-start(bf16[4,112,640]{2,1,0:T(8,128)(2,1)S(1)} %slice.106.refs_0_), channel_id=1, source_target_pairs={{0,4},{2,6},{4,0},{6,2},{8,12},{10,14},{12,8},{14,10},{16,20},{18,... | collective-permute-start | bytes 1720328 | tf_op jit(solution)/shard_map/ppermute | solution.py:90
  77.1 29.3 %collective-permute-start.12 = (bf16[4,104,640]{2,1,0:T(8,128)(2,1)S(1)}, bf16[4,104,640]{2,1,0:T(8,128)(2,1)S(1)}, u32[]{:S(2)}, u32[]{:S(2)}) collective-permute-start(bf16[4,104,640]{2,1,0:T(8,128)(2,1)S(1)} %slice.107.refs_4_), channel_id=1, source_target_pairs={{0,4},{2,6},{4,0},{6,2},{8,12},{10,14},{12,8},{14,10},{16,20},{18,... | collective-permute-start | bytes 1597448 | tf_op jit(solution)/shard_map/ppermute | solution.py:90
  77.4 37.9 %collective-permute-start.13 = (bf16[4,104,640]{2,1,0:T(8,128)(2,1)S(1)}, bf16[4,104,640]{2,1,0:T(8,128)(2,1)}, u32[]{:S(2)}, u32[]{:S(2)}) collective-permute-start(bf16[4,104,640]{2,1,0:T(8,128)(2,1)S(1)} %slice.107.refs_4_), channel_id=1, source_target_pairs={{0,2},{2,0},{4,6},{6,4},{8,10},{10,8},{12,14},{14,12},{16,18},{18,... | collective-permute-start | bytes 1597448 | tf_op jit(solution)/shard_map/ppermute | solution.py:90
  79.3 20.0 %copy-start.59 = (f32[16,1,1152]{2,0,1:T(8,128)}, f32[16,1,1152]{2,0,1:T(8,128)S(1)}, u32[]{:S(2)}) copy-start(f32[16,1,1152]{2,0,1:T(8,128)S(1)} %copy.244) | copy-start | bytes 221188
  97.3 28.8 %collective-permute-start.11 = (bf16[4,112,640]{2,1,0:T(8,128)(2,1)S(1)}, bf16[4,112,640]{2,1,0:T(8,128)(2,1)S(1)}, u32[]{:S(2)}, u32[]{:S(2)}) collective-permute-start(bf16[4,112,640]{2,1,0:T(8,128)(2,1)S(1)} %collective-permute-done.9.refs_1_), channel_id=1, source_target_pairs={{0,4},{2,6},{4,0},{6,2},{8,12},{10,14},{12,8},{14,10},{16,20},{18,... | collective-permute-start | bytes 1720328 | tf_op jit(solution)/shard_map/ppermute | solution.py:90
  101.5 12.4 %all-to-all-start = ((f32[16,1,432]{2,1,0:T(1,128)}), f32[16,1,432]{2,1,0:T(1,128)S(1)}, u32[]{:S(2)}, u32[]{:S(2)}) async-start(f32[16,1,432]{2,1,0:T(1,128)} %copy.182), calls=%async_computation | async-start | bytes 65536 | tf_op jit(solution)/shard_map/all_to_all | solution.py:514
  106.3 283.0 %reduce-scatter.7.cloned.1.call-start = ((), (), s32[]{:S(2)}) async-start(), calls=%async_computation.7 | async-start | bytes 13271040
  106.4 19.8 %collective-permute-start.14 = (bf16[4,104,640]{2,1,0:T(8,128)(2,1)S(1)}, bf16[4,104,640]{2,1,0:T(8,128)(2,1)}, u32[]{:S(2)}, u32[]{:S(2)}) collective-permute-start(bf16[4,104,640]{2,1,0:T(8,128)(2,1)S(1)} %collective-permute-done.12.refs_5_), channel_id=1, source_target_pairs={{0,2},{2,0},{4,6},{6,4},{8,10},{10,8},{12,14},{14,12},{16,18},{18,... | collective-permute-start | bytes 1597448 | tf_op jit(solution)/shard_map/ppermute | solution.py:90
  108.4 24.2 %copy-start.71 = (f32[512]{0:T(512)}, f32[512]{0:T(512)S(1)}, u32[]{:S(2)}) copy-start(f32[512]{0:T(512)S(1)} %fusion.80) | copy-start | bytes 6148
  113.9 1.2 collective-permute-start.7
  132.5 9.2 %collective-permute-start.15 = (bf16[3,576,640]{2,1,0:T(8,128)(2,1)}, bf16[3,576,640]{2,1,0:T(8,128)(2,1)}, u32[]{:S(2)}, u32[]{:S(2)}) collective-permute-start(bf16[3,576,640]{2,1,0:T(8,128)(2,1)} %dynamic-slice_bitcast_fusion), channel_id=1, source_target_pairs={{0,1},{1,0},{2,3},{3,2},{4,5},{5,4},{6,7},{7,6},{8,9},{9,8},{10,11... | collective-permute-start | bytes 6635528 | tf_op jit(solution)/shard_map/ppermute | solution.py:58
  138.1 3.2 collective-permute-start.8
  193.9 4.6 collective-permute-start.18
  196.9 11.8 %copy-start.10 = (bf16[16,144,1152]{2,1,0:T(8,128)(2,1)}, bf16[16,144,1152]{2,1,0:T(8,128)(2,1)S(1)}, u32[]{:S(2)}) copy-start(bf16[16,144,1152]{2,1,0:T(8,128)(2,1)S(1)} %slice.108) | copy-start | bytes 15925252
  202.1 6.4 %collective-permute-start.19 = (bf16[512,1152]{1,0:T(8,128)(2,1)S(1)}, bf16[512,1152]{1,0:T(8,128)(2,1)S(1)}, u32[]{:S(2)}, u32[]{:S(2)}) collective-permute-start(bf16[512,1152]{1,0:T(8,128)(2,1)S(1)} %fusion.45), channel_id=1, source_target_pairs={{0,1},{1,0},{2,3},{3,2},{4,5},{5,4},{6,7},{7,6},{8,9},{9,8},{10,11... | collective-permute-start | bytes 3538952 | tf_op jit(solution)/shard_map/ppermute | solution.py:58
  208.4 10.8 %slice-start.2 = ((s8[5308416]{0:T(1024)(128)(4,1)}), s8[4194304]{0:T(1024)(128)(4,1)S(1)}, s32[]{:S(2)}) async-start(s8[5308416]{0:T(1024)(128)(4,1)} %bitcast.322), calls=%async_computation.10 | async-start | bytes 8388608
  208.6 10.6 %copy-start.42 = (bf16[1024,1152]{1,0:T(8,128)(2,1)}, bf16[1024,1152]{1,0:T(8,128)(2,1)S(1)}, u32[]{:S(2)}) copy-start(bf16[1024,1152]{1,0:T(8,128)(2,1)S(1)} %pad_maximum_fusion.6) | copy-start | bytes 7077892
  208.6 10.6 %slice-start.3 = ((s8[5308416]{0:T(1024)(128)(4,1)}), s8[1114112]{0:T(1024)(128)(4,1)S(1)}, s32[]{:S(2)}) async-start(s8[5308416]{0:T(1024)(128)(4,1)} %bitcast.322), calls=%async_computation.11 | async-start | bytes 2228224
  223.9 7.9 %collective-permute-start.20 = (f32[512,1152]{1,0:T(8,128)}, f32[512,1152]{1,0:T(8,128)}, u32[]{:S(2)}, u32[]{:S(2)}) collective-permute-start(f32[512,1152]{1,0:T(8,128)} %fusion.28), channel_id=1, source_target_pairs={{0,1},{1,0},{2,3},{3,2},{4,5},{5,4},{6,7},{7,6},{8,9},{9,8},{10,11... | collective-permute-start | bytes 7077896 | tf_op jit(solution)/shard_map/ppermute | solution.py:58
  231.9 11.2 %slice-start.8 = ((s8[4718592]{0:T(1024)(128)(4,1)}), s8[4194304]{0:T(1024)(128)(4,1)S(1)}, s32[]{:S(2)}) async-start(s8[4718592]{0:T(1024)(128)(4,1)} %bitcast.367), calls=%async_computation.16 | async-start | bytes 8388608
  239.9 3.0 collective-permute-start.21
  275.2 5.4 %collective-permute-start.22 = (f32[512,1152]{1,0:T(8,128)S(1)}, f32[512,1152]{1,0:T(8,128)S(1)}, u32[]{:S(2)}, u32[]{:S(2)}) collective-permute-start(f32[512,1152]{1,0:T(8,128)S(1)} %fusion.18), channel_id=1, source_target_pairs={{0,1},{1,0},{2,3},{3,2},{4,5},{5,4},{6,7},{7,6},{8,9},{9,8},{10,11... | collective-permute-start | bytes 7077896 | tf_op jit(solution)/shard_map/ppermute | solution.py:58
  288.4 2.9 collective-permute-start.23
  294.8 28.5 %copy-start.39 = (bf16[1024,1280]{0,1:T(8,128)(2,1)S(1)}, bf16[1024,1280]{0,1:T(8,128)(2,1)}, u32[]{:S(2)}) copy-start(bf16[1024,1280]{0,1:T(8,128)(2,1)} %copy-done.38) | copy-start | bytes 7864324
  329.8 7.5 %collective-permute-start.24 = (bf16[3,576,640]{2,1,0:T(8,128)(2,1)}, bf16[3,576,640]{2,1,0:T(8,128)(2,1)S(1)}, u32[]{:S(2)}, u32[]{:S(2)}) collective-permute-start(bf16[3,576,640]{2,1,0:T(8,128)(2,1)} %bitcast.55), channel_id=1, source_target_pairs={{0,1},{1,0},{2,3},{3,2},{4,5},{5,4},{6,7},{7,6},{8,9},{9,8},{10,11... | collective-permute-start | bytes 6635528 | tf_op jit(solution)/shard_map/ppermute | solution.py:58
  348.8 5.1 %collective-permute-start.25 = (f32[512,1280]{1,0:T(8,128)S(1)}, f32[512,1280]{1,0:T(8,128)S(1)}, u32[]{:S(2)}, u32[]{:S(2)}) collective-permute-start(f32[512,1280]{1,0:T(8,128)S(1)} %fusion.32), channel_id=1, source_target_pairs={{0,1},{1,0},{2,3},{3,2},{4,5},{5,4},{6,7},{7,6},{8,9},{9,8},{10,11... | collective-permute-start | bytes 7864328 | tf_op jit(solution)/shard_map/ppermute | solution.py:58
  349.3 35.6 %collective-permute-start.31 = (bf16[4,144,640]{2,1,0:T(8,128)(2,1)}, bf16[4,144,640]{2,1,0:T(8,128)(2,1)}, u32[]{:S(2)}, u32[]{:S(2)}) collective-permute-start(bf16[4,144,640]{2,1,0:T(8,128)(2,1)} %pad_maximum_fusion.13.refs_3_), channel_id=1, source_target_pairs={{0,4},{2,6},{4,0},{6,2},{8,12},{10,14},{12,8},{14,10},{16,20},{18,... | collective-permute-start | bytes 2211848 | tf_op jit(solution)/shard_map/ppermute | solution.py:90
  350.7 35.5 %collective-permute-start.28 = (bf16[4,144,640]{2,1,0:T(8,128)(2,1)}, bf16[4,144,640]{2,1,0:T(8,128)(2,1)}, u32[]{:S(2)}, u32[]{:S(2)}) collective-permute-start(bf16[4,144,640]{2,1,0:T(8,128)(2,1)} %get-tuple-element.81.refs_1_), channel_id=1, source_target_pairs={{0,2},{2,0},{4,6},{6,4},{8,10},{10,8},{12,14},{14,12},{16,18},{18,... | collective-permute-start | bytes 2211848 | tf_op jit(solution)/shard_map/ppermute | solution.py:90
  367.2 1.3 collective-permute-start.26
  371.9 14.4 %all-to-all-start.1 = ((bf16[16,2,216]{2,1,0:T(2,128)(2,1)}), bf16[16,2,216]{2,1,0:T(2,128)(2,1)S(1)}, u32[]{:S(2)}, u32[]{:S(2)}) async-start(bf16[16,2,216]{2,1,0:T(2,128)(2,1)} %reshape.542), calls=%async_computation.1 | async-start | bytes 32768 | tf_op jit(solution)/shard_map/all_to_all | solution.py:636
  376.5 104.2 %reduce-scatter.5.cloned.1.call-start = ((), (), s32[]{:S(2)}) async-start(), calls=%async_computation.5 | async-start | bytes 3317760 | tf_op jit(solution)/shard_map/reduce_scatter | solution.py:274
  376.6 45.7 %collective-permute-start.30 = (bf16[4,144,640]{2,1,0:T(8,128)(2,1)}, bf16[4,144,640]{2,1,0:T(8,128)(2,1)}, u32[]{:S(2)}, u32[]{:S(2)}) collective-permute-start(bf16[4,144,640]{2,1,0:T(8,128)(2,1)} %pad_maximum_fusion.14.refs_4_), channel_id=1, source_target_pairs={{0,4},{2,6},{4,0},{6,2},{8,12},{10,14},{12,8},{14,10},{16,20},{18,... | collective-permute-start | bytes 2211848 | tf_op jit(solution)/shard_map/ppermute | solution.py:90
  378.6 41.0 %collective-permute-start.27 = (bf16[4,144,640]{2,1,0:T(8,128)(2,1)}, bf16[4,144,640]{2,1,0:T(8,128)(2,1)}, u32[]{:S(2)}, u32[]{:S(2)}) collective-permute-start(bf16[4,144,640]{2,1,0:T(8,128)(2,1)} %get-tuple-element.80.refs_2_), channel_id=1, source_target_pairs={{0,2},{2,0},{4,6},{6,4},{8,10},{10,8},{12,14},{14,12},{16,18},{18,... | collective-permute-start | bytes 2211848 | tf_op jit(solution)/shard_map/ppermute | solution.py:90
  397.1 11.4 %copy-start.50 = (f32[576,432]{0,1:T(8,128)S(1)}, f32[576,432]{0,1:T(8,128)}, u32[]{:S(2)}) copy-start(f32[576,432]{0,1:T(8,128)} %param.36) | copy-start | bytes 2985988
  397.1 11.4 %copy-start.51 = (f32[576,432]{0,1:T(8,128)S(1)}, f32[576,432]{0,1:T(8,128)}, u32[]{:S(2)}) copy-start(f32[576,432]{0,1:T(8,128)} %param.31) | copy-start | bytes 2985988
  397.1 11.4 %copy-start.60 = (f32[16,1,1152]{2,0,1:T(8,128)S(1)}, f32[16,1,1152]{2,0,1:T(8,128)}, u32[]{:S(2)}) copy-start(f32[16,1,1152]{2,0,1:T(8,128)} %copy-done.59) | copy-start | bytes 221188
  397.1 25.2 %collective-permute-start.32 = (bf16[4,144,640]{2,1,0:T(8,128)(2,1)}, bf16[4,144,640]{2,1,0:T(8,128)(2,1)}, u32[]{:S(2)}, u32[]{:S(2)}) collective-permute-start(bf16[4,144,640]{2,1,0:T(8,128)(2,1)} %shard_map.360), channel_id=1, source_target_pairs={{0,2},{2,0},{4,6},{6,4},{8,10},{10,8},{12,14},{14,12},{16,18},{18,... | collective-permute-start | bytes 2211848 | tf_op jit(solution)/shard_map/ppermute | solution.py:90
  399.1 20.4 %collective-permute-start.29 = (bf16[4,144,640]{2,1,0:T(8,128)(2,1)}, bf16[4,144,640]{2,1,0:T(8,128)(2,1)}, u32[]{:S(2)}, u32[]{:S(2)}) collective-permute-start(bf16[4,144,640]{2,1,0:T(8,128)(2,1)} %shard_map.358), channel_id=1, source_target_pairs={{0,4},{2,6},{4,0},{6,2},{8,12},{10,14},{12,8},{14,10},{16,20},{18,... | collective-permute-start | bytes 2211848 | tf_op jit(solution)/shard_map/ppermute | solution.py:90
  400.7 18.2 %all-to-all-start.2 = ((f32[16,1,704]{2,1,0:T(1,128)}), f32[16,1,704]{2,1,0:T(1,128)S(1)}, u32[]{:S(2)}, u32[]{:S(2)}) async-start(f32[16,1,704]{2,1,0:T(1,128)} %copy.203), calls=%async_computation.2 | async-start | bytes 98304 | tf_op jit(solution)/shard_map/all_to_all | solution.py:296
  410.7 11.5 %copy-start.45 = (bf16[4,72,640]{2,1,0:T(8,128)(2,1)S(1)}, bf16[4,72,640]{2,1,0:T(8,128)(2,1)}, u32[]{:S(2)}) copy-start(bf16[4,72,640]{2,1,0:T(8,128)(2,1)} %get-tuple-element.88) | copy-start | bytes 1105924
  410.8 11.5 %copy-start.46 = (bf16[4,72,640]{2,1,0:T(8,128)(2,1)S(1)}, bf16[4,72,640]{2,1,0:T(8,128)(2,1)}, u32[]{:S(2)}) copy-start(bf16[4,72,640]{2,1,0:T(8,128)(2,1)} %get-tuple-element.129) | copy-start | bytes 1105924
  424.9 3.4 collective-permute-start.33
  424.9 24.6 %collective-permute-start.34 = (bf16[2,144,640]{2,1,0:T(8,128)(2,1)S(1)}, bf16[2,144,640]{2,1,0:T(8,128)(2,1)S(1)}, u32[]{:S(2)}, u32[]{:S(2)}) collective-permute-start(bf16[2,144,640]{2,1,0:T(8,128)(2,1)S(1)} %dynamic-slice_bitcast_fusion.4), channel_id=1, source_target_pairs={{0,8},{2,10},{4,12},{6,14},{8,0},{10,2},{12,4},{14,6},{16,24},{18,... | collective-permute-start | bytes 1105928 | tf_op jit(solution)/shard_map/ppermute | solution.py:90
  427.3 37.7 %collective-permute-start.36 = (bf16[2,144,640]{2,1,0:T(8,128)(2,1)}, bf16[2,144,640]{2,1,0:T(8,128)(2,1)S(1)}, u32[]{:S(2)}, u32[]{:S(2)}) collective-permute-start(bf16[2,144,640]{2,1,0:T(8,128)(2,1)} %dynamic-slice_bitcast_fusion.3), channel_id=1, source_target_pairs={{0,8},{2,10},{4,12},{6,14},{8,0},{10,2},{12,4},{14,6},{16,24},{18,... | collective-permute-start | bytes 1105928 | tf_op jit(solution)/shard_map/ppermute | solution.py:90
  450.3 27.9 %copy-start.44 = (f32[576,216]{0,1:T(8,128)S(1)}, f32[576,216]{0,1:T(8,128)}, u32[]{:S(2)}) copy-start(f32[576,216]{0,1:T(8,128)} %param.27) | copy-start | bytes 1492996
  450.3 27.9 %copy-start.58 = (f32[576,216]{0,1:T(8,128)S(1)}, f32[576,216]{0,1:T(8,128)}, u32[]{:S(2)}) copy-start(f32[576,216]{0,1:T(8,128)} %param.37) | copy-start | bytes 1492996
  451.5 16.1 %collective-permute-start.35 = (bf16[1,144,640]{2,1,0:T(8,128)(2,1)S(1)}, bf16[1,144,640]{2,1,0:T(8,128)(2,1)S(1)}, u32[]{:S(2)}, u32[]{:S(2)}) collective-permute-start(bf16[1,144,640]{2,1,0:T(8,128)(2,1)S(1)} %constant_dynamic-slice_fusion.3), channel_id=1, source_target_pairs={{0,16},{2,18},{4,20},{6,22},{8,24},{10,26},{12,28},{14,30},{16,0},... | collective-permute-start | bytes 552968 | tf_op jit(solution)/shard_map/ppermute | solution.py:90
  466.8 11.4 %collective-permute-start.37 = (bf16[1,144,640]{2,1,0:T(8,128)(2,1)S(1)}, bf16[1,144,640]{2,1,0:T(8,128)(2,1)S(1)}, u32[]{:S(2)}, u32[]{:S(2)}) collective-permute-start(bf16[1,144,640]{2,1,0:T(8,128)(2,1)S(1)} %constant_dynamic-slice_fusion.2), channel_id=1, source_target_pairs={{0,16},{2,18},{4,20},{6,22},{8,24},{10,26},{12,28},{14,30},{16,0},... | collective-permute-start | bytes 552968 | tf_op jit(solution)/shard_map/ppermute | solution.py:90
  481.9 3.3 collective-permute-start.39
  484.7 6.6 %collective-permute-start.38 = (bf16[144,576]{1,0:T(8,128)(2,1)}, bf16[144,576]{1,0:T(8,128)(2,1)}, u32[]{:S(2)}, u32[]{:S(2)}) collective-permute-start(bf16[144,576]{1,0:T(8,128)(2,1)} %bitcast.284), channel_id=1, source_target_pairs={{0,1},{1,0},{2,3},{3,2},{4,5},{5,4},{6,7},{7,6},{8,9},{9,8},{10,11... | collective-permute-start | bytes 497672 | tf_op jit(solution)/shard_map/ppermute | solution.py:58
  (82 other events, 320.1 us)
Sparse Core Ops, SparseCore 0:
  17.4 171.9 all-gather.3
  268.8 120.5 reduce-scatter.6
  391.6 70.6 reduce-scatter.4

commit v2 on v1

--- a/solution.py
+++ b/solution.py
@@ -658,13 +658,15 @@
         contraction_sum = narrow(mlp_sum[:cut_c], proj_share).reshape(proj_share, seq_size, -1)
         contraction_sum = by_distance(contraction_sum, 1)
     expansion_sum = mlp_sum[cut_c:]
-    waits = ([back],)
-    attention_sum = jnp.concatenate([part.finish(*waits) for part in attention_sum], axis=0)
     expansion_sum = around(
         by_distance(expansion_sum.reshape(hidden_piece, seq_size, row_share), 1)
     )
-    expansion_sum = jnp.concatenate(in_order(expansion_sum), axis=0).T
-    contraction_sum = jnp.stack(in_order(around(contraction_sum)), axis=0).reshape(
+    expansion_sum = jnp.concatenate(in_order(expansion_sum), axis=0)
+    contraction_sum = jnp.stack(in_order(around(contraction_sum)), axis=0)
+    waits = [back], [expansion_sum, contraction_sum]
+    attention_sum = jnp.concatenate([part.finish(*waits) for part in attention_sum], axis=0)
+    expansion_sum = expansion_sum.T
+    contraction_sum = contraction_sum.reshape(
         seq_size, proj_share, dp_size // seq_size, hidden_piece
     )
     contraction_sum = jnp.transpose(contraction_sum, (2, 0, 3, 1)).reshape(

time: 511 us -> 506 us (level)
  waiting for transfers between devices: 150 us -> 136 us
  blocking collectives: 0 us -> 12.1 us
  starting transfers between devices: 57.3 us -> 48.6 us
    ppermute x22, waiting for transfers between devices: 114 us -> 89.3 us  [swap(): return lax.ppermute(array, 'dp', [(j, j ^ bit) for j in range(size)])]
    all_to_all x0 -> x1, blocking collectives: none -> 12.1 us  [body(): lax.all_to_all(mod_grad, 'dp', 0, 0, tiled=True)]
    all_to_all x1, waiting for transfers between devices: 5.45 us -> 11.6 us  [body(): mod_part = lax.all_to_all(mod_part, 'dp', 0, 0, tiled=True)]
    all_to_all x1, waiting for transfers between devices: 8.16 us -> 13.6 us  [sum_small(): return jnp.sum(lax.all_to_all(blocks, 'dp', 0, 0, tiled=True), axis=0)]
  transfers between devices with their start and end apart: 46 -> 45, of which waited for: 24 -> 22; matrix products, arithmetic and copies ran while one was open for 29% -> 29% of each run, Pallas kernels for 11% -> 11%
where the time goes in v2:
time: 506 us; the launch traced here: 496 us
  waiting for transfers between devices  136 us (27%)
  matrix products  92.1 us (18%)
  other arithmetic  76.1 us (15%)
  local copies, waits for them, and re-layouts  60 us (12%)
  Pallas kernels  53 us (10%)
  starting transfers between devices  48.6 us (10%)
  between operations  18.1 us (4%)
  blocking collectives  12.1 us (2%)
    dot_general x21, matrix products, dot(): lax.dot_general(first, second, (over, ((), ())), preferred_element_type=j...  92.1 us
    ppermute x22, waiting for transfers between devices, swap(): return lax.ppermute(array, 'dp', [(j, j ^ bit) for j in range(size)])  89.3 us
    ppermute x22, starting transfers between devices, swap(): return lax.ppermute(array, 'dp', [(j, j ^ bit) for j in range(size)])  35.6 us
    pallas_call x1, Pallas kernels, attend_back(): pl.pallas_call(lambda *refs: softmax_back_kernel(heads, head_size, math.g...  28.4 us
    pallas_call x1, Pallas kernels, attend(): pl.pallas_call(lambda *refs: softmax_kernel(heads, head_size, math.gcd(le...  22.2 us
    unnamed x210, local copies, waits for them, and re-layouts  20.5 us
    all_to_all x1, waiting for transfers between devices, sum_small(): return jnp.sum(lax.all_to_all(blocks, 'dp', 0, 0, tiled=True), axis=0)  13.6 us
    ppermute x18, waiting for transfers between devices, around(): got[(size - r) % size] = lax.ppermute(pieces[r], 'seq', steps)  12.6 us
  transfers between devices with their start and end apart: 45, of which 22 were waited for; matrix products, arithmetic and copies ran while one was open for 29% of the time, Pallas kernels for 11%

profile of v2, /device:TPU:0, one launch (start us, length us, event | category | flops | bytes accessed | tf_op | source)
XLA Modules:
  0.0 495.7 jit_solution(9550179215198531703)
XLA Ops:
  18.3 3.7 collective-permute-start.3
  23.8 1.9 collective-permute-done.1
  27.4 12.8 %collective-permute-done.3 = bf16[1,216,640]{2,1,0:T(8,128)(2,1)S(1)} collective-permute-done((bf16[1,216,640]{2,1,0:T(8,128)(2,1)S(1)}, bf16[1,216,640]{2,1,0:T(8,128)(2,1)S(1)}, u32[]{:S(2)}, u32[]{:S(2)}) %collective-permute-start.3) | collective-permute-done | bytes 276512 | tf_op jit(solution)/shard_map/ppermute | solution.py:90
  40.3 5.3 %collective-permute-start.4 = (bf16[2,216,640]{2,1,0:T(8,128)(2,1)S(1)}, bf16[2,216,640]{2,1,0:T(8,128)(2,1)S(1)}, u32[]{:S(2)}, u32[]{:S(2)}) collective-permute-start(bf16[2,216,640]{2,1,0:T(8,128)(2,1)S(1)} %maximum_bitcast_fusion), channel_id=1, source_target_pairs={{0,8},{2,10},{4,12},{6,14},{8,0},{10,2},{12,4},{14,6},{16,24},{18,... | collective-permute-start | bytes 1658888 | tf_op jit(solution)/shard_map/ppermute | solution.py:90
  46.3 16.9 %collective-permute-done.4 = bf16[2,216,640]{2,1,0:T(8,128)(2,1)S(1)} collective-permute-done((bf16[2,216,640]{2,1,0:T(8,128)(2,1)S(1)}, bf16[2,216,640]{2,1,0:T(8,128)(2,1)S(1)}, u32[]{:S(2)}, u32[]{:S(2)}) %collective-permute-start.4) | collective-permute-done | bytes 552992 | tf_op jit(solution)/shard_map/ppermute | solution.py:90
  64.5 4.5 collective-permute-done.5
  69.8 6.8 %collective-permute-start.6 = (bf16[8,2,1156]{2,1,0:T(2,128)(2,1)S(1)}, bf16[8,2,1156]{2,1,0:T(2,128)(2,1)S(1)}, u32[]{:S(2)}, u32[]{:S(2)}) collective-permute-start(bf16[8,2,1156]{2,1,0:T(2,128)(2,1)S(1)} %pad_maximum_fusion.19), channel_id=1, source_target_pairs={{0,16},{2,18},{4,20},{6,22},{8,24},{10,26},{12,28},{14,30},{16,0},... | collective-permute-start | bytes 110984 | tf_op jit(solution)/shard_map/ppermute | solution.py:90
  79.4 1.9 collective-permute-start.13
  82.3 15.2 %collective-permute-done.9.refs_1_ = bf16[4,112,640]{2,1,0:T(8,128)(2,1)S(1)} collective-permute-done((bf16[4,112,640]{2,1,0:T(8,128)(2,1)S(1)}, bf16[4,112,640]{2,1,0:T(8,128)(2,1)S(1)}, u32[]{:S(2)}, u32[]{:S(2)}) %collective-permute-start.9) | collective-permute-done | bytes 573472 | tf_op jit(solution)/shard_map/ppermute | solution.py:90
  101.2 4.6 all-to-all-start
  105.8 2.0 collective-permute-start.14
  107.8 11.6 %all-to-all-done = f32[16,1,432]{2,1,0:T(1,128)S(1)} async-done(((f32[16,1,432]{2,1,0:T(1,128)}), f32[16,1,432]{2,1,0:T(1,128)S(1)}, u32[]{:S(2)}, u32[]{:S(2)}) %all-to-all-start) | async-done | bytes 27680 | tf_op jit(solution)/shard_map/all_to_all | solution.py:514
  120.9 7.0 %collective-permute-done.14.refs_7_ = bf16[4,104,640]{2,1,0:T(8,128)(2,1)} collective-permute-done((bf16[4,104,640]{2,1,0:T(8,128)(2,1)S(1)}, bf16[4,104,640]{2,1,0:T(8,128)(2,1)}, u32[]{:S(2)}, u32[]{:S(2)}) %collective-permute-start.14) | collective-permute-done | bytes 532512 | tf_op jit(solution)/shard_map/ppermute | solution.py:90
  127.9 2.4 shard_map.349
  130.7 2.1 copy-done.18
  136.0 2.4 copy.190
  140.5 2.7 collective-permute-done.8
  143.6 3.0 bitcast_select_fusion.1
  146.9 2.1 copy-done.32
  149.0 6.6 %fusion.9.refs_0_ = bf16[1,1024,1728]{2,1,0:T(8,128)(2,1)} fusion(bf16[1024,1280]{0,1:T(8,128)(2,1)S(1)} %pad_maximum_fusion.5, bf16[1728,1280]{1,0:T(8,128)(2,1)S(1)} %bitcast.331), kind=kOutput, calls=%fused_computation.28 | convolution fusion | flops 4531617792 | bytes 10584064 | tf_op jit(solution)/shard_map/dot_general | solution.py:38
  155.6 22.2 %shard_map.350 = (f32[1,1024,576]{2,1,0:T(8,128)S(1)}, bf16[1,1024,576]{2,1,0:T(8,128)(2,1)S(1)}, f32[1,8,1024]{2,1,0:T(8,128)S(1)}) custom-call(bf16[1,1024,1728]{2,1,0:T(8,128)(2,1)} %fusion.9.refs_0_), custom_call_target="tpu_custom_call" | custom-call | flops 2415919104 | bytes 83886080 | tf_op jit(solution)/shard_map/pallas_call | solution.py:324
  180.9 8.6 %all-gather.4.cloned.1.call-done.refs_0_ = bf16[16,324,1152]{2,1,0:T(8,128)(2,1)} async-done(((bf16[1,324,1152]{2,1,0:T(8,128)(2,1)}), bf16[16,324,1152]{2,1,0:T(8,128)(2,1)}) %all-gather.4.cloned.1.call-update) | async-done | bytes 11943952 | tf_op jit(solution)/shard_map/all_gather | solution.py:485
  189.6 1.8 fusion.96
  194.1 2.9 slice.108
  202.7 3.0 fusion.95
  205.6 2.9 pad_maximum_fusion.1
  208.7 10.6 %fusion.2 = (bf16[1024,2304]{1,0:T(8,128)(2,1)}, bf16[1024,2304]{1,0:T(8,128)(2,1)S(1)}) fusion(bf16[1024,1152]{1,0:T(8,128)(2,1)S(1)} %pad_maximum_fusion.6, bf16[2304,1152]{1,0:T(8,128)(2,1)S(1)} %bitcast.293), kind=kOutput, calls=%fused_computation.6 | convolution fusion | flops 5471207424 | bytes 17104896 | tf_op jit(solution)/shard_map/dot_general | solution.py:38
  219.4 4.7 fusion.28
  225.3 6.6 %fusion.30 = f32[512,1152]{1,0:T(8,128)S(1)} fusion(bf16[1152,2304]{1,0:T(8,128)(2,1)} %bitcast.319, bf16[1024,2304]{1,0:T(8,128)(2,1)} %copy-done.86), kind=kOutput, calls=%fused_computation.67 | convolution fusion | flops 2717908992 | bytes 10027008 | tf_op jit(solution)/shard_map/dot_general | solution.py:38
  232.0 3.6 fusion.17
  235.7 4.2 fusion.22
  240.5 2.5 collective-permute-done.21
  243.3 3.3 convolution_convert_fusion.2
  246.6 3.8 convolution_convert_fusion.1
  250.5 6.5 %multiply_convert_fusion = bf16[1024,2304]{1,0:T(8,128)(2,1)S(1)} fusion(bf16[1024,2304]{1,0:T(8,128)(2,1)S(1)} %bitcast.369, bf16[1024,1152]{1,0:T(8,128)(2,1)S(1)} %pad_maximum_fusion.7, bf16[1152,2304]{1,0:T(8,128)(2,1)S(1)} %bitcast.325), kind=kOutput, calls=%fused_computation.7 | convolution fusion | flops 5442895872 | bytes 17104896 | tf_op jit(solution)/shard_map/dot_general | solution.py:38
  257.0 6.7 %convolution_convert_fusion = bf16[2304,1152]{1,0:T(8,128)(2,1)S(1)} fusion(bf16[1024,2304]{1,0:T(8,128)(2,1)S(1)} %multiply_convert_fusion, bf16[1024,1152]{1,0:T(8,128)(2,1)S(1)} %copy-done.42), kind=kOutput, calls=%fused_computation.1 | convolution fusion | flops 5438472192 | bytes 12386304 | tf_op jit(solution)/shard_map/dot_general | solution.py:38
  263.7 5.0 %copy_bitcast_fusion.refs_1_ = bf16[4,4,288,1152]{3,2,1,0:T(8,128)(2,1)} fusion(bf16[4,4,144,1152]{3,2,1,0:T(8,128)(2,1)S(1)} %bitcast.327, bf16[4,4,72,1152]{3,2,1,0:T(8,128)(2,1)S(1)} %bitcast.339, bf16[4,4,72,1152]{3,2,1,0:T(8,128)(2,1)S(1)} %bitcast.338), kind=kLoop, calls=%fused_computation.3 | loop fusion | flops 31850496 | bytes 21233664 | tf_op jit(solution)/shard_map/transpose | solution.py:258
  268.9 6.6 %fusion.18 = f32[512,1152]{1,0:T(8,128)S(1)} fusion(bf16[2304,1152]{1,0:T(8,128)(2,1)} %shard_map.354, bf16[1024,2304]{1,0:T(8,128)(2,1)} %copy-done.87), kind=kOutput, calls=%fused_computation.41 | convolution fusion | flops 2717908992 | bytes 10027008 | tf_op jit(solution)/shard_map/dot_general | solution.py:38
  275.9 4.9 fusion.20
  288.7 2.8 collective-permute-done.23
  291.7 3.2 fusion.39.refs_1_
  295.0 28.4 %shard_map.355 = bf16[1,1024,1728]{2,1,0:T(8,128)(2,1)} custom-call(bf16[1,1024,1728]{2,1,0:T(8,128)(2,1)} %fusion.9.refs_0_, bf16[1,1024,576]{2,1,0:T(8,128)(2,1)} %fusion.39.refs_1_, f32[1,1024,576]{2,1,0:T(8,128)} %copy-done.2, f32[1,8,1024]{2,1,0:T(8,128)} %copy-done.3), custom_call_target="tpu_custom_call" | custom-call | tf_op jit(solution)/shard_map/pallas_call | solution.py:392
  323.4 6.6 %convolution_convert_fusion.5 = bf16[1728,640]{1,0:T(8,128)(2,1)} fusion(bf16[1024,2,640]{0,2,1:T(8,128)(2,1)S(1)} %bitcast.340, s32[]{:T(128)S(6)} %select_n.309, bf16[1,1024,1728]{2,1,0:T(8,128)(2,1)} %shard_map.355), kind=kOutput, calls=%fused_computation.30 | convolution fusion | flops 2266030080 | bytes 7061508 | tf_op jit(solution)/shard_map/dot_general | solution.py:38
  330.0 4.4 convolution_convert_fusion.4
  334.4 3.1 convolution_convert_fusion.6
  343.6 5.5 %fusion.32 = f32[512,1280]{1,0:T(8,128)S(1)} fusion(bf16[1728,1280]{1,0:T(8,128)(2,1)} %bitcast.332, bf16[1024,1728]{1,0:T(8,128)(2,1)} %shard_map.356), kind=kOutput, calls=%fused_computation.76 | convolution fusion | flops 2264924160 | bytes 8880128 | tf_op jit(solution)/shard_map/dot_general | solution.py:38
  349.7 2.5 fusion.34
  352.3 2.0 collective-permute-done.25
  354.5 2.3 copy.223
  356.8 4.2 fusion.97
  361.0 2.1 copy.207
  372.3 12.1 %all_to_all.19 = bf16[16,2,216]{2,1,0:T(2,128)(2,1)S(1)} all-to-all(bf16[16,2,216]{2,1,0:T(2,128)(2,1)} %reshape.542), channel_id=1, replica_groups=mesh['dp'=16,'seq'=2] {'dp'}, dimensions={0} | all-to-all | bytes 27648 | tf_op jit(solution)/shard_map/all_to_all | solution.py:636
  390.6 15.7 %collective-permute-done.31.refs_0_ = bf16[4,144,640]{2,1,0:T(8,128)(2,1)} collective-permute-done((bf16[4,144,640]{2,1,0:T(8,128)(2,1)}, bf16[4,144,640]{2,1,0:T(8,128)(2,1)}, u32[]{:S(2)}, u32[]{:S(2)}) %collective-permute-start.31) | collective-permute-done | bytes 737312 | tf_op jit(solution)/shard_map/ppermute | solution.py:90
  407.0 2.6 fusion.36.refs_0_
  409.5 2.4 add_convert_fusion.2.refs_0_
  411.9 2.2 add_add_fusion.2
  417.8 3.7 all-to-all-start.2
  421.5 2.3 add_multiply_fusion
  423.8 13.6 %all-to-all-done.2 = f32[16,1,704]{2,1,0:T(1,128)S(1)} async-done(((f32[16,1,704]{2,1,0:T(1,128)}), f32[16,1,704]{2,1,0:T(1,128)S(1)}, u32[]{:S(2)}, u32[]{:S(2)}) %all-to-all-start.2) | async-done | bytes 45088 | tf_op jit(solution)/shard_map/all_to_all | solution.py:296
  438.0 2.7 fusion.38.refs_1_
  440.8 2.6 add_convert_fusion.1.refs_2_
  448.9 5.9 %collective-permute-done.34.refs_0_ = bf16[2,144,640]{2,1,0:T(8,128)(2,1)S(1)} collective-permute-done((bf16[2,144,640]{2,1,0:T(8,128)(2,1)S(1)}, bf16[2,144,640]{2,1,0:T(8,128)(2,1)S(1)}, u32[]{:S(2)}, u32[]{:S(2)}) %collective-permute-start.34) | collective-permute-done | bytes 368672 | tf_op jit(solution)/shard_map/ppermute | solution.py:90
  458.2 6.4 %collective-permute-done.38.refs_0_ = bf16[2,144,640]{2,1,0:T(8,128)(2,1)S(1)} collective-permute-done((bf16[2,144,640]{2,1,0:T(8,128)(2,1)S(1)}, bf16[2,144,640]{2,1,0:T(8,128)(2,1)S(1)}, u32[]{:S(2)}, u32[]{:S(2)}) %collective-permute-start.38) | collective-permute-done | bytes 368672 | tf_op jit(solution)/shard_map/ppermute | solution.py:90
  481.1 3.0 add_multiply_fusion.1
  (431 shorter events, 109.8 us)
Async XLA Ops:
  7.2 182.4 %all-gather.4.cloned.1.call-start = ((), (), s32[]{:S(2)}) async-start(), calls=%async_computation.6 | async-start | bytes 12847104 | tf_op jit(solution)/shard_map/all_gather | solution.py:485
  12.8 2.7 collective-permute-start.16
  15.0 1.5 collective-permute-start.17
  15.7 7.9 %copy-start.7 = (bf16[1,512,1152]{2,1,0:T(8,128)(2,1)S(1)}, bf16[1,512,1152]{2,1,0:T(8,128)(2,1)}, u32[]{:S(2)}) copy-start(bf16[1,512,1152]{2,1,0:T(8,128)(2,1)} %param.21) | copy-start | bytes 3538948
  17.8 4.2 collective-permute-start
  18.3 21.8 %collective-permute-start.3 = (bf16[1,216,640]{2,1,0:T(8,128)(2,1)S(1)}, bf16[1,216,640]{2,1,0:T(8,128)(2,1)S(1)}, u32[]{:S(2)}, u32[]{:S(2)}) collective-permute-start(bf16[1,216,640]{2,1,0:T(8,128)(2,1)S(1)} %get-tuple-element.112), channel_id=1, source_target_pairs={{0,16},{2,18},{4,20},{6,22},{8,24},{10,26},{12,28},{14,30},{16,0},... | collective-permute-start | bytes 829448 | tf_op jit(solution)/shard_map/ppermute | solution.py:90
  22.0 3.7 collective-permute-start.1
  25.8 19.8 %collective-permute-start.2 = (bf16[2,2,1156]{2,1,0:T(2,128)(2,1)S(1)}, bf16[2,2,1156]{2,1,0:T(2,128)(2,1)S(1)}, u32[]{:S(2)}, u32[]{:S(2)}) collective-permute-start(bf16[2,2,1156]{2,1,0:T(2,128)(2,1)S(1)} %pad_maximum_fusion.21), channel_id=1, source_target_pairs={{0,4},{2,6},{4,0},{6,2},{8,12},{10,14},{12,8},{14,10},{16,20},{18,... | collective-permute-start | bytes 27752 | tf_op jit(solution)/shard_map/ppermute | solution.py:90
  40.3 22.8 %collective-permute-start.4 = (bf16[2,216,640]{2,1,0:T(8,128)(2,1)S(1)}, bf16[2,216,640]{2,1,0:T(8,128)(2,1)S(1)}, u32[]{:S(2)}, u32[]{:S(2)}) collective-permute-start(bf16[2,216,640]{2,1,0:T(8,128)(2,1)S(1)} %maximum_bitcast_fusion), channel_id=1, source_target_pairs={{0,8},{2,10},{4,12},{6,14},{8,0},{10,2},{12,4},{14,6},{16,24},{18,... | collective-permute-start | bytes 1658888 | tf_op jit(solution)/shard_map/ppermute | solution.py:90
  64.5 12.6 %copy-start.25 = (bf16[2,2,216,640]{3,2,1,0:T(8,128)(2,1)S(1)}, bf16[2,2,216,640]{3,2,1,0:T(8,128)(2,1)}, u32[]{:S(2)}) copy-start(bf16[2,2,216,640]{3,2,1,0:T(8,128)(2,1)} %copy.188) | copy-start | bytes 3317764
  64.5 4.5 collective-permute-start.5
  64.5 69.9 %copy-start.67 = (f32[512]{0:T(512)}, f32[512]{0:T(512)S(1)}, u32[]{:S(2)}) copy-start(f32[512]{0:T(512)S(1)} %broadcast_multiply_fusion.2) | copy-start | bytes 6148
  69.8 49.6 %copy-start.85 = (s32[2,4]{1,0:T(2,128)S(1)}, s32[2,4]{1,0:T(2,128)}, u32[]{:S(2)}) copy-start(s32[2,4]{1,0:T(2,128)} %constant.189.clone) | copy-start | bytes 100
  69.8 12.3 %collective-permute-start.6 = (bf16[8,2,1156]{2,1,0:T(2,128)(2,1)S(1)}, bf16[8,2,1156]{2,1,0:T(2,128)(2,1)S(1)}, u32[]{:S(2)}, u32[]{:S(2)}) collective-permute-start(bf16[8,2,1156]{2,1,0:T(2,128)(2,1)S(1)} %pad_maximum_fusion.19), channel_id=1, source_target_pairs={{0,16},{2,18},{4,20},{6,22},{8,24},{10,26},{12,28},{14,30},{16,0},... | collective-permute-start | bytes 110984 | tf_op jit(solution)/shard_map/ppermute | solution.py:90
  77.1 42.4 %copy-start.77 = (f32[512]{0:T(512)}, f32[512]{0:T(512)S(1)}, u32[]{:S(2)}) copy-start(f32[512]{0:T(512)S(1)} %fusion.15) | copy-start | bytes 6148
  77.2 20.3 %collective-permute-start.9 = (bf16[4,112,640]{2,1,0:T(8,128)(2,1)S(1)}, bf16[4,112,640]{2,1,0:T(8,128)(2,1)S(1)}, u32[]{:S(2)}, u32[]{:S(2)}) collective-permute-start(bf16[4,112,640]{2,1,0:T(8,128)(2,1)S(1)} %slice.106.refs_0_), channel_id=1, source_target_pairs={{0,2},{2,0},{4,6},{6,4},{8,10},{10,8},{12,14},{14,12},{16,18},{18,... | collective-permute-start | bytes 1720328 | tf_op jit(solution)/shard_map/ppermute | solution.py:90
  77.3 43.6 %collective-permute-start.10 = (bf16[4,112,640]{2,1,0:T(8,128)(2,1)S(1)}, bf16[4,112,640]{2,1,0:T(8,128)(2,1)S(1)}, u32[]{:S(2)}, u32[]{:S(2)}) collective-permute-start(bf16[4,112,640]{2,1,0:T(8,128)(2,1)S(1)} %slice.106.refs_0_), channel_id=1, source_target_pairs={{0,4},{2,6},{4,0},{6,2},{8,12},{10,14},{12,8},{14,10},{16,20},{18,... | collective-permute-start | bytes 1720328 | tf_op jit(solution)/shard_map/ppermute | solution.py:90
  78.3 27.5 %collective-permute-start.12 = (bf16[4,104,640]{2,1,0:T(8,128)(2,1)S(1)}, bf16[4,104,640]{2,1,0:T(8,128)(2,1)S(1)}, u32[]{:S(2)}, u32[]{:S(2)}) collective-permute-start(bf16[4,104,640]{2,1,0:T(8,128)(2,1)S(1)} %slice.107.refs_4_), channel_id=1, source_target_pairs={{0,4},{2,6},{4,0},{6,2},{8,12},{10,14},{12,8},{14,10},{16,20},{18,... | collective-permute-start | bytes 1597448 | tf_op jit(solution)/shard_map/ppermute | solution.py:90
  79.4 41.5 %collective-permute-start.13 = (bf16[4,104,640]{2,1,0:T(8,128)(2,1)S(1)}, bf16[4,104,640]{2,1,0:T(8,128)(2,1)}, u32[]{:S(2)}, u32[]{:S(2)}) collective-permute-start(bf16[4,104,640]{2,1,0:T(8,128)(2,1)S(1)} %slice.107.refs_4_), channel_id=1, source_target_pairs={{0,2},{2,0},{4,6},{6,4},{8,10},{10,8},{12,14},{14,12},{16,18},{18,... | collective-permute-start | bytes 1597448 | tf_op jit(solution)/shard_map/ppermute | solution.py:90
  82.3 16.7 %copy-start.59 = (f32[16,1,1152]{2,0,1:T(8,128)}, f32[16,1,1152]{2,0,1:T(8,128)S(1)}, u32[]{:S(2)}) copy-start(f32[16,1,1152]{2,0,1:T(8,128)S(1)} %copy.248) | copy-start | bytes 221188
  97.5 30.5 %collective-permute-start.11 = (bf16[4,112,640]{2,1,0:T(8,128)(2,1)S(1)}, bf16[4,112,640]{2,1,0:T(8,128)(2,1)S(1)}, u32[]{:S(2)}, u32[]{:S(2)}) collective-permute-start(bf16[4,112,640]{2,1,0:T(8,128)(2,1)S(1)} %collective-permute-done.9.refs_1_), channel_id=1, source_target_pairs={{0,4},{2,6},{4,0},{6,2},{8,12},{10,14},{12,8},{14,10},{16,20},{18,... | collective-permute-start | bytes 1720328 | tf_op jit(solution)/shard_map/ppermute | solution.py:90
  101.2 18.2 %all-to-all-start = ((f32[16,1,432]{2,1,0:T(1,128)}), f32[16,1,432]{2,1,0:T(1,128)S(1)}, u32[]{:S(2)}, u32[]{:S(2)}) async-start(f32[16,1,432]{2,1,0:T(1,128)} %copy.189), calls=%async_computation | async-start | bytes 65536 | tf_op jit(solution)/shard_map/all_to_all | solution.py:514
  105.8 280.7 %reduce-scatter.7.cloned.1.call-start = ((), (), s32[]{:S(2)}) async-start(), calls=%async_computation.7 | async-start | bytes 13271040
  105.8 22.1 %collective-permute-start.14 = (bf16[4,104,640]{2,1,0:T(8,128)(2,1)S(1)}, bf16[4,104,640]{2,1,0:T(8,128)(2,1)}, u32[]{:S(2)}, u32[]{:S(2)}) collective-permute-start(bf16[4,104,640]{2,1,0:T(8,128)(2,1)S(1)} %collective-permute-done.12.refs_5_), channel_id=1, source_target_pairs={{0,2},{2,0},{4,6},{6,4},{8,10},{10,8},{12,14},{14,12},{16,18},{18,... | collective-permute-start | bytes 1597448 | tf_op jit(solution)/shard_map/ppermute | solution.py:90
  107.8 26.6 %copy-start.71 = (f32[512]{0:T(512)}, f32[512]{0:T(512)S(1)}, u32[]{:S(2)}) copy-start(f32[512]{0:T(512)S(1)} %fusion.80) | copy-start | bytes 6148
  119.4 1.2 collective-permute-start.7
  134.3 9.2 %collective-permute-start.15 = (bf16[3,576,640]{2,1,0:T(8,128)(2,1)}, bf16[3,576,640]{2,1,0:T(8,128)(2,1)}, u32[]{:S(2)}, u32[]{:S(2)}) collective-permute-start(bf16[3,576,640]{2,1,0:T(8,128)(2,1)} %dynamic-slice_bitcast_fusion), channel_id=1, source_target_pairs={{0,1},{1,0},{2,3},{3,2},{4,5},{5,4},{6,7},{7,6},{8,9},{9,8},{10,11... | collective-permute-start | bytes 6635528 | tf_op jit(solution)/shard_map/ppermute | solution.py:58
  134.5 9.1 %slice-start = ((s8[4423680]{0:T(1024)(128)(4,1)}), s8[229376]{0:T(1024)(128)(4,1)S(1)}, s32[]{:S(2)}) async-start(s8[4423680]{0:T(1024)(128)(4,1)} %bitcast.296), calls=%async_computation.8 | async-start | bytes 458752
  139.9 3.2 collective-permute-start.8
  194.0 4.6 collective-permute-start.18
  197.0 11.7 %copy-start.10 = (bf16[16,144,1152]{2,1,0:T(8,128)(2,1)}, bf16[16,144,1152]{2,1,0:T(8,128)(2,1)S(1)}, u32[]{:S(2)}) copy-start(bf16[16,144,1152]{2,1,0:T(8,128)(2,1)S(1)} %slice.108) | copy-start | bytes 15925252
  202.2 6.3 %collective-permute-start.19 = (bf16[512,1152]{1,0:T(8,128)(2,1)S(1)}, bf16[512,1152]{1,0:T(8,128)(2,1)S(1)}, u32[]{:S(2)}, u32[]{:S(2)}) collective-permute-start(bf16[512,1152]{1,0:T(8,128)(2,1)S(1)} %fusion.45), channel_id=1, source_target_pairs={{0,1},{1,0},{2,3},{3,2},{4,5},{5,4},{6,7},{7,6},{8,9},{9,8},{10,11... | collective-permute-start | bytes 3538952 | tf_op jit(solution)/shard_map/ppermute | solution.py:58
  208.5 10.9 %slice-start.2 = ((s8[5308416]{0:T(1024)(128)(4,1)}), s8[4194304]{0:T(1024)(128)(4,1)S(1)}, s32[]{:S(2)}) async-start(s8[5308416]{0:T(1024)(128)(4,1)} %bitcast.320), calls=%async_computation.10 | async-start | bytes 8388608
  208.7 10.7 %copy-start.41 = (bf16[1024,1152]{1,0:T(8,128)(2,1)}, bf16[1024,1152]{1,0:T(8,128)(2,1)S(1)}, u32[]{:S(2)}) copy-start(bf16[1024,1152]{1,0:T(8,128)(2,1)S(1)} %pad_maximum_fusion.6) | copy-start | bytes 7077892
  208.7 10.7 %slice-start.3 = ((s8[5308416]{0:T(1024)(128)(4,1)}), s8[1114112]{0:T(1024)(128)(4,1)S(1)}, s32[]{:S(2)}) async-start(s8[5308416]{0:T(1024)(128)(4,1)} %bitcast.320), calls=%async_computation.11 | async-start | bytes 2228224
  224.0 7.9 %collective-permute-start.20 = (f32[512,1152]{1,0:T(8,128)}, f32[512,1152]{1,0:T(8,128)}, u32[]{:S(2)}, u32[]{:S(2)}) collective-permute-start(f32[512,1152]{1,0:T(8,128)} %fusion.28), channel_id=1, source_target_pairs={{0,1},{1,0},{2,3},{3,2},{4,5},{5,4},{6,7},{7,6},{8,9},{9,8},{10,11... | collective-permute-start | bytes 7077896 | tf_op jit(solution)/shard_map/ppermute | solution.py:58
  232.0 11.2 %slice-start.8 = ((s8[4718592]{0:T(1024)(128)(4,1)}), s8[4194304]{0:T(1024)(128)(4,1)S(1)}, s32[]{:S(2)}) async-start(s8[4718592]{0:T(1024)(128)(4,1)} %bitcast.366), calls=%async_computation.16 | async-start | bytes 8388608
  235.7 7.6 %slice-start.9 = ((s8[4718592]{0:T(1024)(128)(4,1)}), s8[524288]{0:T(1024)(128)(4,1)S(1)}, s32[]{:S(2)}) async-start(s8[4718592]{0:T(1024)(128)(4,1)} %bitcast.366), calls=%async_computation.17 | async-start | bytes 1048576
  240.0 3.0 collective-permute-start.21
  268.8 197.7 %reduce-scatter.5.cloned.1.call-start = ((), (), s32[]{:S(2)}) async-start(), calls=%async_computation.5 | async-start | bytes 3317760 | tf_op jit(solution)/shard_map/reduce_scatter | solution.py:274
  275.4 5.4 %collective-permute-start.22 = (f32[512,1152]{1,0:T(8,128)S(1)}, f32[512,1152]{1,0:T(8,128)S(1)}, u32[]{:S(2)}, u32[]{:S(2)}) collective-permute-start(f32[512,1152]{1,0:T(8,128)S(1)} %fusion.18), channel_id=1, source_target_pairs={{0,1},{1,0},{2,3},{3,2},{4,5},{5,4},{6,7},{7,6},{8,9},{9,8},{10,11... | collective-permute-start | bytes 7077896 | tf_op jit(solution)/shard_map/ppermute | solution.py:58
  288.6 2.9 collective-permute-start.23
  295.0 28.5 %copy-start.38 = (bf16[1024,1280]{0,1:T(8,128)(2,1)S(1)}, bf16[1024,1280]{0,1:T(8,128)(2,1)}, u32[]{:S(2)}) copy-start(bf16[1024,1280]{0,1:T(8,128)(2,1)} %copy-done.37) | copy-start | bytes 7864324
  330.0 7.5 %collective-permute-start.24 = (bf16[3,576,640]{2,1,0:T(8,128)(2,1)}, bf16[3,576,640]{2,1,0:T(8,128)(2,1)S(1)}, u32[]{:S(2)}, u32[]{:S(2)}) collective-permute-start(bf16[3,576,640]{2,1,0:T(8,128)(2,1)} %bitcast.54), channel_id=1, source_target_pairs={{0,1},{1,0},{2,3},{3,2},{4,5},{5,4},{6,7},{7,6},{8,9},{9,8},{10,11... | collective-permute-start | bytes 6635528 | tf_op jit(solution)/shard_map/ppermute | solution.py:58
  349.1 5.1 %collective-permute-start.25 = (f32[512,1280]{1,0:T(8,128)S(1)}, f32[512,1280]{1,0:T(8,128)S(1)}, u32[]{:S(2)}, u32[]{:S(2)}) collective-permute-start(f32[512,1280]{1,0:T(8,128)S(1)} %fusion.32), channel_id=1, source_target_pairs={{0,1},{1,0},{2,3},{3,2},{4,5},{5,4},{6,7},{7,6},{8,9},{9,8},{10,11... | collective-permute-start | bytes 7864328 | tf_op jit(solution)/shard_map/ppermute | solution.py:58
  367.5 1.3 collective-permute-start.26
  386.5 20.4 %copy-start.83 = (f32[512]{0:T(512)S(1)}, f32[512]{0:T(512)}, u32[]{:S(2)}) copy-start(f32[512]{0:T(512)} %get-tuple-element.35) | copy-start | bytes 6148
  386.5 19.8 %collective-permute-start.31 = (bf16[4,144,640]{2,1,0:T(8,128)(2,1)}, bf16[4,144,640]{2,1,0:T(8,128)(2,1)}, u32[]{:S(2)}, u32[]{:S(2)}) collective-permute-start(bf16[4,144,640]{2,1,0:T(8,128)(2,1)} %pad_maximum_fusion.13.refs_3_), channel_id=1, source_target_pairs={{0,4},{2,6},{4,0},{6,2},{8,12},{10,14},{12,8},{14,10},{16,20},{18,... | collective-permute-start | bytes 2211848 | tf_op jit(solution)/shard_map/ppermute | solution.py:90
  387.2 19.7 %collective-permute-start.28 = (bf16[4,144,640]{2,1,0:T(8,128)(2,1)}, bf16[4,144,640]{2,1,0:T(8,128)(2,1)}, u32[]{:S(2)}, u32[]{:S(2)}) collective-permute-start(bf16[4,144,640]{2,1,0:T(8,128)(2,1)} %get-tuple-element.81.refs_1_), channel_id=1, source_target_pairs={{0,2},{2,0},{4,6},{6,4},{8,10},{10,8},{12,14},{14,12},{16,18},{18,... | collective-permute-start | bytes 2211848 | tf_op jit(solution)/shard_map/ppermute | solution.py:90
  387.7 53.0 %collective-permute-start.30 = (bf16[4,144,640]{2,1,0:T(8,128)(2,1)}, bf16[4,144,640]{2,1,0:T(8,128)(2,1)}, u32[]{:S(2)}, u32[]{:S(2)}) collective-permute-start(bf16[4,144,640]{2,1,0:T(8,128)(2,1)} %pad_maximum_fusion.14.refs_4_), channel_id=1, source_target_pairs={{0,4},{2,6},{4,0},{6,2},{8,12},{10,14},{12,8},{14,10},{16,20},{18,... | collective-permute-start | bytes 2211848 | tf_op jit(solution)/shard_map/ppermute | solution.py:90
  389.2 48.8 %collective-permute-start.27 = (bf16[4,144,640]{2,1,0:T(8,128)(2,1)}, bf16[4,144,640]{2,1,0:T(8,128)(2,1)}, u32[]{:S(2)}, u32[]{:S(2)}) collective-permute-start(bf16[4,144,640]{2,1,0:T(8,128)(2,1)} %get-tuple-element.80.refs_2_), channel_id=1, source_target_pairs={{0,2},{2,0},{4,6},{6,4},{8,10},{10,8},{12,14},{14,12},{16,18},{18,... | collective-permute-start | bytes 2211848 | tf_op jit(solution)/shard_map/ppermute | solution.py:90
  414.1 7.4 %copy-start.60 = (f32[16,1,1152]{2,0,1:T(8,128)S(1)}, f32[16,1,1152]{2,0,1:T(8,128)}, u32[]{:S(2)}) copy-start(f32[16,1,1152]{2,0,1:T(8,128)} %copy-done.59) | copy-start | bytes 221188
  414.1 26.6 %collective-permute-start.32 = (bf16[4,144,640]{2,1,0:T(8,128)(2,1)}, bf16[4,144,640]{2,1,0:T(8,128)(2,1)}, u32[]{:S(2)}, u32[]{:S(2)}) collective-permute-start(bf16[4,144,640]{2,1,0:T(8,128)(2,1)} %shard_map.360), channel_id=1, source_target_pairs={{0,2},{2,0},{4,6},{6,4},{8,10},{10,8},{12,14},{14,12},{16,18},{18,... | collective-permute-start | bytes 2211848 | tf_op jit(solution)/shard_map/ppermute | solution.py:90
  414.7 23.3 %collective-permute-start.29 = (bf16[4,144,640]{2,1,0:T(8,128)(2,1)}, bf16[4,144,640]{2,1,0:T(8,128)(2,1)}, u32[]{:S(2)}, u32[]{:S(2)}) collective-permute-start(bf16[4,144,640]{2,1,0:T(8,128)(2,1)} %shard_map.358), channel_id=1, source_target_pairs={{0,4},{2,6},{4,0},{6,2},{8,12},{10,14},{12,8},{14,10},{16,20},{18,... | collective-permute-start | bytes 2211848 | tf_op jit(solution)/shard_map/ppermute | solution.py:90
  417.8 19.6 %all-to-all-start.2 = ((f32[16,1,704]{2,1,0:T(1,128)}), f32[16,1,704]{2,1,0:T(1,128)S(1)}, u32[]{:S(2)}, u32[]{:S(2)}) async-start(f32[16,1,704]{2,1,0:T(1,128)} %copy.209), calls=%async_computation.2 | async-start | bytes 98304 | tf_op jit(solution)/shard_map/all_to_all | solution.py:296
  423.8 16.9 %copy-start.44 = (bf16[4,72,640]{2,1,0:T(8,128)(2,1)S(1)}, bf16[4,72,640]{2,1,0:T(8,128)(2,1)}, u32[]{:S(2)}) copy-start(bf16[4,72,640]{2,1,0:T(8,128)(2,1)} %get-tuple-element.88) | copy-start | bytes 1105924
  423.8 16.9 %copy-start.45 = (bf16[4,72,640]{2,1,0:T(8,128)(2,1)S(1)}, bf16[4,72,640]{2,1,0:T(8,128)(2,1)}, u32[]{:S(2)}) copy-start(bf16[4,72,640]{2,1,0:T(8,128)(2,1)} %get-tuple-element.131) | copy-start | bytes 1105924
  443.3 2.3 collective-permute-start.33
  443.4 11.4 %collective-permute-start.34 = (bf16[2,144,640]{2,1,0:T(8,128)(2,1)S(1)}, bf16[2,144,640]{2,1,0:T(8,128)(2,1)S(1)}, u32[]{:S(2)}, u32[]{:S(2)}) collective-permute-start(bf16[2,144,640]{2,1,0:T(8,128)(2,1)S(1)} %dynamic-slice_bitcast_fusion.4), channel_id=1, source_target_pairs={{0,8},{2,10},{4,12},{6,14},{8,0},{10,2},{12,4},{14,6},{16,24},{18,... | collective-permute-start | bytes 1105928 | tf_op jit(solution)/shard_map/ppermute | solution.py:90
  444.5 20.2 %collective-permute-start.38 = (bf16[2,144,640]{2,1,0:T(8,128)(2,1)S(1)}, bf16[2,144,640]{2,1,0:T(8,128)(2,1)S(1)}, u32[]{:S(2)}, u32[]{:S(2)}) collective-permute-start(bf16[2,144,640]{2,1,0:T(8,128)(2,1)S(1)} %dynamic-slice_bitcast_fusion.3), channel_id=1, source_target_pairs={{0,8},{2,10},{4,12},{6,14},{8,0},{10,2},{12,4},{14,6},{16,24},{18,... | collective-permute-start | bytes 1105928 | tf_op jit(solution)/shard_map/ppermute | solution.py:90
  457.3 19.4 %collective-permute-start.35 = (bf16[1,144,640]{2,1,0:T(8,128)(2,1)}, bf16[1,144,640]{2,1,0:T(8,128)(2,1)S(1)}, u32[]{:S(2)}, u32[]{:S(2)}) collective-permute-start(bf16[1,144,640]{2,1,0:T(8,128)(2,1)} %constant_dynamic-slice_fusion.3), channel_id=1, source_target_pairs={{0,16},{2,18},{4,20},{6,22},{8,24},{10,26},{12,28},{14,30},{16,0},... | collective-permute-start | bytes 552968 | tf_op jit(solution)/shard_map/ppermute | solution.py:90
  467.7 3.1 collective-permute-start.37
  468.5 11.6 %collective-permute-start.39 = (bf16[1,144,640]{2,1,0:T(8,128)(2,1)}, bf16[1,144,640]{2,1,0:T(8,128)(2,1)}, u32[]{:S(2)}, u32[]{:S(2)}) collective-permute-start(bf16[1,144,640]{2,1,0:T(8,128)(2,1)} %constant_dynamic-slice_fusion), channel_id=1, source_target_pairs={{0,16},{2,18},{4,20},{6,22},{8,24},{10,26},{12,28},{14,30},{16,0},... | collective-permute-start | bytes 552968 | tf_op jit(solution)/shard_map/ppermute | solution.py:90
  470.4 3.7 collective-permute-start.36
  (81 other events, 283.1 us)
Sparse Core Ops, SparseCore 0:
  17.7 171.7 all-gather.3
  268.9 102.8 reduce-scatter.6
  386.6 49.7 reduce-scatter.4
